TPU v7x, 256 devices: a whole 4x4x8 slice. The times are simulated.
256 devices in a mesh: node: 16 (over z_lo, y), local: 16 (over x, z_hi, core).
Axes of the slice: x: 4, y: 4, z: 8 (z_hi: 2, z_lo: 4; z = z_hi * 4 + z_lo), core: 2. Of those that a mesh axis runs over, the one named last changes fastest.
Arguments:
- activations: bfloat16 [65536, 5120], P(('node', 'local')), may hold values from -6 to 6
- queries: bfloat16 [65536, 5120], P(('node', 'local')), may hold values from -100 to 100
- rotated_key_value: bfloat16 [65536, 2048], P(('node', 'local')), may hold values from -5 to 5
- attention_out_grad: bfloat16 [65536, 5120], P(('node', 'local')), may hold values from -6 to 6
- adapter_down: bfloat16 [5120, 128], replicated, may hold values from -0.078125 to 0.078125
- adapter_up: bfloat16 [128, 1024], replicated, may hold values from -0.75 to 0.75
- bin_local_index: int32 [256, 256], P(('node', 'local')), may hold values from 0 to 15, as said below
- bin_row_offset: int32 [256, 256], P(('node', 'local')), may hold values from 0 to 3, as said below
- spill_node: int32 [256, 256], P(('node', 'local')), may hold values from 0 to 15, as said below
- spill_row_offset: int32 [256, 256], P(('node', 'local')), may hold values from 0 to 3, as said below
- arrival_pick_index: int32 [256, 256], P(('node', 'local')), may hold values from 0 to 383, as said below
- packed_sequence_number: int32 [256, 256], P(('node', 'local')), may hold values from 0 to 7, never falling along the last dimension, each value on 1 to 128 neighbouring positions
Outputs:
- key_value_cotangent: bfloat16 [65536, 2048], P(('node', 'local'))
- down_factor_grad: float32 [5120, 128], P(('node', 'local'))
- up_factor_grad_transposed: float32 [1024, 128], P(('node', 'local'))
Inputs may be any that keep to these rules, and one draw needn't show every extreme that they name: `bin_local_index`: rows that stay or overflow carry the device's own local index. At most 4 rows of a device go to one other bin of its node, and that bin sends back exactly as many to it; in every node one device sends 4 rows to every other bin of the node. `bin_row_offset`: offsets of the rows one device sends to one bin are 0 up to their count minus 1; zero for other rows. `spill_node`: A row moves across nodes only if it stays in its node's bin of its own local index otherwise; at most 4 rows of a device go to one other node, and as many come back; for every local index one node sends 4 rows to every other node. Rows that do not overflow carry their own node. `spill_row_offset`: offsets of the overflow rows one device sends to one node are 0 up to their count minus 1; zero for other rows. `arrival_pick_index`: every bin holds exactly 256 rows: each row of the arrival list of 384 entries that is filled is named once, and no empty entry is named.
All inputs are finite; a program needn't handle non-finite values.
Results may differ from a plain program's by a relative error of at most 0.0056.
Values may be sent and summed in bfloat16 or wider, within the bound.
No kernel may reach another device: no remote copies, remote signals or barrier semaphores. Data moves between devices by JAX's collectives and lax.ppermute only.
A program may use at most 128 MiB of HBM per device.

v0:
```python
import math

import jax
import jax.numpy as jnp
from jax import lax
from jax.sharding import PartitionSpec as P

KV_HEADS = 8
HEAD = 128
ADAPTER_RANK = 64
CAP_L = 4
CAP_N = 4
GROUP = 5
KEY_HEAD_WIDTH = 1024


rope_theta = 1000000.0


def rope_tables(segments):
    slot_ids = jnp.arange(segments.shape[0], dtype=jnp.int32)
    seg_start = jnp.sum((segments[None, :] < segments[:, None]).astype(jnp.int32), axis=1)
    position = (slot_ids - seg_start).astype(jnp.float32)
    frequency = rope_theta ** (-jnp.arange(0, HEAD, 2).astype(jnp.float32) / HEAD)
    angles = position[:, None] * frequency[None, :]
    return (jnp.cos(angles), jnp.sin(angles))


def unrotate(key_rot, cosine_table, sine_table):
    half_head = HEAD // 2
    first_half = key_rot[..., :half_head]
    second_half = key_rot[..., half_head:]
    cos_rows = cosine_table[:, None, :]
    sin_rows = sine_table[:, None, :]
    return jnp.concatenate(
        [
            first_half * cos_rows + second_half * sin_rows,
            second_half * cos_rows - first_half * sin_rows,
        ],
        axis=-1,
    )


def attention_backward(query_rows, kv_rows, grad_rows, segments):
    row_count = query_rows.shape[0]
    score_scale = 1.0 / math.sqrt(HEAD)
    slot_ids = jnp.arange(row_count, dtype=jnp.int32)
    allowed = (segments[:, None] == segments[None, :]) & (slot_ids[None, :] <= slot_ids[:, None])
    query_groups = query_rows.reshape(row_count, KV_HEADS, GROUP * HEAD)
    grad_groups = grad_rows.reshape(row_count, KV_HEADS, GROUP * HEAD)
    key_heads = kv_rows[:, :KEY_HEAD_WIDTH].reshape(row_count, KV_HEADS, HEAD)
    value_heads = kv_rows[:, KEY_HEAD_WIDTH:].reshape(row_count, KV_HEADS, HEAD)

    def per_group(group_id):
        query_block = lax.dynamic_index_in_dim(query_groups, group_id, 1, keepdims=False).reshape(
            row_count, GROUP, HEAD
        )
        grad_block = lax.dynamic_index_in_dim(grad_groups, group_id, 1, keepdims=False).reshape(
            row_count, GROUP, HEAD
        )
        key_block = lax.dynamic_index_in_dim(key_heads, group_id, 1, keepdims=False)
        value_block = lax.dynamic_index_in_dim(value_heads, group_id, 1, keepdims=False)
        scores = (
            jnp.einsum("isd,jd->sij", query_block, key_block, preferred_element_type=jnp.float32)
            * score_scale
        )
        scores = jnp.where(allowed[None], scores, -jnp.inf)
        row_max = jnp.max(scores, axis=-1, keepdims=True)
        weights = jnp.exp(scores - row_max)
        probs = weights / jnp.sum(weights, axis=-1, keepdims=True)
        prob_grad = jnp.einsum(
            "isd,jd->sij", grad_block, value_block, preferred_element_type=jnp.float32
        )
        row_delta = jnp.sum(probs * prob_grad, axis=-1, keepdims=True)
        score_grad = (probs * (prob_grad - row_delta)).astype(jnp.bfloat16)
        value_cotangent_rows = jnp.einsum(
            "sij,isd->jd",
            probs.astype(jnp.bfloat16),
            grad_block,
            preferred_element_type=jnp.float32,
        )
        key_rot = (
            jnp.einsum("sij,isd->jd", score_grad, query_block, preferred_element_type=jnp.float32)
            * score_scale
        )
        return (key_rot, value_cotangent_rows)

    key_rot, value_cotangent_rows = lax.map(per_group, jnp.arange(KV_HEADS, dtype=jnp.int32))
    key_rot = jnp.transpose(key_rot, (1, 0, 2))
    value_cotangent_rows = jnp.transpose(value_cotangent_rows, (1, 0, 2))
    cosine_table, sine_table = rope_tables(segments)
    key_cotangent_rows = unrotate(key_rot, cosine_table, sine_table)
    return jnp.concatenate(
        [
            key_cotangent_rows.reshape(row_count, KEY_HEAD_WIDTH),
            value_cotangent_rows.reshape(row_count, KEY_HEAD_WIDTH),
        ],
        axis=1,
    ).astype(jnp.bfloat16)


def adapter_terms(active_rows, key_value_cotangent, adapter_down, adapter_up):
    key_cotangent_rows = key_value_cotangent[:, :KEY_HEAD_WIDTH]
    value_cotangent_rows = key_value_cotangent[:, KEY_HEAD_WIDTH:]
    raise_key = jnp.dot(
        key_cotangent_rows, adapter_up[:ADAPTER_RANK].T, preferred_element_type=jnp.float32
    )
    raise_value = jnp.dot(
        value_cotangent_rows, adapter_up[ADAPTER_RANK:].T, preferred_element_type=jnp.float32
    )
    lift = jnp.concatenate([raise_key, raise_value], axis=1).astype(jnp.bfloat16)
    down_factor_grad = jnp.dot(active_rows.T, lift, preferred_element_type=jnp.float32)
    down_product = jnp.dot(active_rows, adapter_down, preferred_element_type=jnp.float32).astype(
        jnp.bfloat16
    )
    up_key = jnp.dot(
        key_cotangent_rows.T, down_product[:, :ADAPTER_RANK], preferred_element_type=jnp.float32
    )
    up_value = jnp.dot(
        value_cotangent_rows.T, down_product[:, ADAPTER_RANK:], preferred_element_type=jnp.float32
    )
    return (down_factor_grad, jnp.concatenate([up_key, up_value], axis=1))


def pack_rows(source_rows, slot_ids, capacity):
    empty_rows = jnp.zeros((capacity, source_rows.shape[1]), source_rows.dtype)
    return empty_rows.at[slot_ids].set(source_rows, mode="drop")


def local(
    activations,
    queries,
    rotated_key_value,
    attention_out_grad,
    adapter_down,
    adapter_up,
    bin_local_index,
    bin_row_offset,
    spill_node,
    spill_row_offset,
    arrival_pick_index,
    packed_sequence_number,
):
    row_count = activations.shape[0]
    local_count = lax.axis_size("local")
    node_count = lax.axis_size("node")
    near_total = local_count * CAP_L
    far_total = node_count * CAP_N
    own_local = lax.axis_index("local")
    own_node = lax.axis_index("node")
    bin_local_index = bin_local_index.reshape(-1)
    bin_row_offset = bin_row_offset.reshape(-1)
    spill_node = spill_node.reshape(-1)
    spill_row_offset = spill_row_offset.reshape(-1)
    arrival_pick_index = arrival_pick_index.reshape(-1)
    segments = packed_sequence_number.reshape(-1)
    moved_in = bin_local_index != own_local
    moved_out = spill_node != own_node
    local_slots = jnp.where(moved_in, bin_local_index * CAP_L + bin_row_offset, near_total)
    node_slots = jnp.where(moved_out, spill_node * CAP_N + spill_row_offset, far_total)

    def assemble(own_rows, near_rows, far_rows):
        arrivals = jnp.concatenate([own_rows, near_rows, far_rows], axis=0)
        return jnp.take(arrivals, arrival_pick_index, axis=0)

    near_rows = (
        lax.all_to_all(
            pack_rows(activations, local_slots, near_total),
            "local",
            split_axis=0,
            concat_axis=0,
            tiled=True,
        ),
        lax.all_to_all(
            pack_rows(queries, local_slots, near_total),
            "local",
            split_axis=0,
            concat_axis=0,
            tiled=True,
        ),
        lax.all_to_all(
            pack_rows(rotated_key_value, local_slots, near_total),
            "local",
            split_axis=0,
            concat_axis=0,
            tiled=True,
        ),
        lax.all_to_all(
            pack_rows(attention_out_grad, local_slots, near_total),
            "local",
            split_axis=0,
            concat_axis=0,
            tiled=True,
        ),
    )
    far_rows = (
        lax.all_to_all(
            pack_rows(activations, node_slots, far_total),
            "node",
            split_axis=0,
            concat_axis=0,
            tiled=True,
        ),
        lax.all_to_all(
            pack_rows(queries, node_slots, far_total),
            "node",
            split_axis=0,
            concat_axis=0,
            tiled=True,
        ),
        lax.all_to_all(
            pack_rows(rotated_key_value, node_slots, far_total),
            "node",
            split_axis=0,
            concat_axis=0,
            tiled=True,
        ),
        lax.all_to_all(
            pack_rows(attention_out_grad, node_slots, far_total),
            "node",
            split_axis=0,
            concat_axis=0,
            tiled=True,
        ),
    )
    active_bin = assemble(activations, near_rows[0], far_rows[0])
    query_bin = assemble(queries, near_rows[1], far_rows[1])
    kv_bin = assemble(rotated_key_value, near_rows[2], far_rows[2])
    grad_bin = assemble(attention_out_grad, near_rows[3], far_rows[3])
    key_value_cotangent = attention_backward(query_bin, kv_bin, grad_bin, segments)
    down_factor_grad, up_factor_grad_transposed = adapter_terms(
        active_bin, key_value_cotangent, adapter_down, adapter_up
    )
    totals = (
        lax.psum_scatter(down_factor_grad, ("node", "local"), scatter_dimension=0, tiled=True),
        lax.psum_scatter(
            up_factor_grad_transposed, ("node", "local"), scatter_dimension=0, tiled=True
        ),
    )
    factor = 1.0 / math.sqrt(row_count * local_count * node_count)
    return (key_value_cotangent, totals[0] * factor, totals[1] * factor)


def solution(mesh):
    placed = (
        P(("node", "local"), None),
        P(("node", "local"), None),
        P(("node", "local"), None),
        P(("node", "local"), None),
        P(),
        P(),
        P(("node", "local"), None),
        P(("node", "local"), None),
        P(("node", "local"), None),
        P(("node", "local"), None),
        P(("node", "local"), None),
        P(("node", "local"), None),
    )
    return jax.shard_map(
        local,
        mesh=mesh,
        in_specs=placed,
        out_specs=(
            P(("node", "local"), None),
            P(("node", "local"), None),
            P(("node", "local"), None),
        ),
        check_vma=False,
    )
```

profile of v0, /device:TPU:2, one launch (start us, length us, event | category | flops | bytes accessed | tf_op | source)
XLA Modules:
  0.0 585.2 jit_solution(7096433973709067225)
XLA Ops:
  8.0 2.8 scatter_custom_fusion.1
  11.6 8.6 %all-to-all-start.1 = ((bf16[16,4,2048]{2,1,0:T(4,128)(2,1)}), bf16[16,4,2048]{2,1,0:T(4,128)(2,1)S(1)}, u32[]{:S(2)}, u32[]{:S(2)}) async-start(bf16[16,4,2048]{2,1,0:T(4,128)(2,1)} %all_to_all.67), calls=%async_computation.1 | async-start | bytes 524288 | tf_op jit(solution)/shard_map/all_to_all | solution.py:211
  24.5 6.4 %all-to-all-done.1 = bf16[16,4,2048]{2,1,0:T(4,128)(2,1)S(1)} async-done(((bf16[16,4,2048]{2,1,0:T(4,128)(2,1)}), bf16[16,4,2048]{2,1,0:T(4,128)(2,1)S(1)}, u32[]{:S(2)}, u32[]{:S(2)}) %all-to-all-start.1) | async-done | bytes 262176 | tf_op jit(solution)/shard_map/all_to_all | solution.py:211
  30.9 8.8 %all-to-all-start = ((bf16[16,4,2048]{2,1,0:T(4,128)(2,1)}), bf16[16,4,2048]{2,1,0:T(4,128)(2,1)S(1)}, u32[]{:S(2)}, u32[]{:S(2)}) async-start(bf16[16,4,2048]{2,1,0:T(4,128)(2,1)} %all_to_all.64), calls=%async_computation | async-start | bytes 524288 | tf_op jit(solution)/shard_map/all_to_all | solution.py:181
  39.7 5.2 scatter_custom_fusion.3
  46.0 3.2 all-to-all-done
  49.2 5.9 %all-to-all-start.3 = ((bf16[16,4,5120]{2,1,0:T(4,128)(2,1)}), bf16[16,4,5120]{2,1,0:T(4,128)(2,1)S(1)}, u32[]{:S(2)}, u32[]{:S(2)}) async-start(bf16[16,4,5120]{2,1,0:T(4,128)(2,1)} %all_to_all.73), calls=%async_computation.3 | async-start | bytes 1310720 | tf_op jit(solution)/shard_map/all_to_all | solution.py:204
  55.1 5.2 scatter_custom_fusion.2
  61.4 11.9 %all-to-all-done.3 = bf16[16,4,5120]{2,1,0:T(4,128)(2,1)S(1)} async-done(((bf16[16,4,5120]{2,1,0:T(4,128)(2,1)}), bf16[16,4,5120]{2,1,0:T(4,128)(2,1)S(1)}, u32[]{:S(2)}, u32[]{:S(2)}) %all-to-all-start.3) | async-done | bytes 655392 | tf_op jit(solution)/shard_map/all_to_all | solution.py:204
  73.3 5.3 all-to-all-start.2
  78.6 5.9 %scatter_custom_fusion.5 = bf16[64,5120]{1,0:T(8,128)(2,1)} fusion(s32[256]{0:T(256)S(1)} %bitcast.149, bf16[256,5120]{1,0:T(8,128)(2,1)} %param.19, bf16[]{:T(256)} %constant.45.clone.1), kind=kCustom, calls=%fused_computation.75 | custom fusion | bytes 655872 | tf_op jit(solution)/shard_map/scatter | solution.py:127
  84.5 5.6 scatter_custom_fusion.4
  90.2 5.9 %scatter_custom_fusion.7 = bf16[64,5120]{1,0:T(8,128)(2,1)} fusion(s32[256]{0:T(256)S(1)} %bitcast.150, bf16[256,5120]{1,0:T(8,128)(2,1)} %param.16, bf16[]{:T(256)} %constant.45.clone.1), kind=kCustom, calls=%fused_computation.71 | custom fusion | bytes 655872 | tf_op jit(solution)/shard_map/scatter | solution.py:127
  96.1 5.9 %scatter_custom_fusion.6 = bf16[64,5120]{1,0:T(8,128)(2,1)} fusion(s32[256]{0:T(256)S(1)} %bitcast.154, bf16[256,5120]{1,0:T(8,128)(2,1)} %param.16, bf16[]{:T(256)} %constant.45.clone.1), kind=kCustom, calls=%fused_computation.73 | custom fusion | bytes 655872 | tf_op jit(solution)/shard_map/scatter | solution.py:127
  110.2 4.9 all-to-all-start.5
  122.0 11.2 %all-to-all-done.5 = bf16[16,4,5120]{2,1,0:T(4,128)(2,1)} async-done(((bf16[16,4,5120]{2,1,0:T(4,128)(2,1)}), bf16[16,4,5120]{2,1,0:T(4,128)(2,1)}, u32[]{:S(2)}, u32[]{:S(2)}) %all-to-all-start.5) | async-done | bytes 655392 | tf_op jit(solution)/shard_map/all_to_all | solution.py:218
  133.2 9.9 %all-to-all-start.4 = ((bf16[16,4,5120]{2,1,0:T(4,128)(2,1)}), bf16[16,4,5120]{2,1,0:T(4,128)(2,1)S(1)}, u32[]{:S(2)}, u32[]{:S(2)}) async-start(bf16[16,4,5120]{2,1,0:T(4,128)(2,1)} %all_to_all.76), calls=%async_computation.4 | async-start | bytes 1310720 | tf_op jit(solution)/shard_map/all_to_all | solution.py:188
  147.1 3.5 pad_maximum_fusion
  150.6 8.8 %gather_fusion.1 = bf16[256,5120]{1,0:T(8,128)(2,1)} fusion(bf16[384,5120]{1,0:T(8,128)(2,1)} %pad_maximum_fusion, s32[1024]{0:T(1024)S(1)} %pad_clamp_fusion), kind=kCustom, calls=%fused_computation.clone | custom fusion | bytes 5243904 | tf_op jit(solution)/shard_map/jit(_take)/gather | solution.py:164
  160.9 2.8 all-to-all-done.4
  163.7 4.5 all-to-all-start.7
  169.1 3.5 pad_maximum_fusion.1
  172.6 8.9 %gather_fusion.2 = bf16[256,5120]{1,0:T(8,128)(2,1)} fusion(bf16[384,5120]{1,0:T(8,128)(2,1)} %pad_maximum_fusion.1, s32[1024]{0:T(1024)S(1)} %pad_clamp_fusion), kind=kCustom, calls=%fused_computation.1.clone | custom fusion | bytes 5243904 | tf_op jit(solution)/shard_map/jit(_take)/gather | solution.py:164
  181.5 5.4 broadcast_select_fusion.1
  186.9 4.4 copy.57
  191.3 4.5 copy.58
  195.7 7.3 %all-to-all-start.6 = ((bf16[16,4,5120]{2,1,0:T(4,128)(2,1)}), bf16[16,4,5120]{2,1,0:T(4,128)(2,1)}, u32[]{:S(2)}, u32[]{:S(2)}) async-start(bf16[16,4,5120]{2,1,0:T(4,128)(2,1)} %all_to_all.82), calls=%async_computation.6 | async-start | bytes 1310720 | tf_op jit(solution)/shard_map/all_to_all | solution.py:167
  203.4 81.4 %while.13 = (s32[]{:T(128)}, f32[8,256,128]{2,1,0:T(8,128)S(1)}, bf16[8,256,128]{2,1,0:T(8,128)(2,1)}, s32[8]{0:T(128)S(1)}, bf16[256,8,128]{2,0,1:T(8,128)(2,1)...) while((s32[]{:T(128)}, f32[8,256,128]{2,1,0:T(8,128)S(1)}, ...), condition=%wide.region_10.12_spmd.clone, body=%wide.region_6.11_spmd.clone.sunk | while | flops 340032512 | bytes 16291535 | solution.py:88
  288.5 3.5 pad_maximum_fusion.2
  292.0 8.8 %gather_fusion.3 = bf16[256,5120]{1,0:T(8,128)(2,1)} fusion(bf16[384,5120]{1,0:T(8,128)(2,1)} %pad_maximum_fusion.2, s32[1024]{0:T(1024)S(1)} %pad_clamp_fusion), kind=kCustom, calls=%fused_computation.2.clone | custom fusion | bytes 5243904 | tf_op jit(solution)/shard_map/jit(_take)/gather | solution.py:164
  300.8 2.9 convolution_convert_fusion
  311.2 264.1 %all-reduce.5.cloned.1.call-done = (f32[5120,128]{1,0:T(8,128)}, f32[1024,128]{0,1:T(8,128)}) async-done(((f32[5120,128]{1,0:T(8,128)}, f32[1024,128]{0,1:T(8,128)}), (f32[5120,128]{1,0:T(8,128)}, f32[1024,128]{0,1:T(8,128)})) %all-reduce.5.cloned.1.call-update) | async-done | bytes 3145744
  (158 shorter events, 109.3 us)
Async XLA Ops:
  7.2 293.7 %copy-start = (bf16[5120,128]{1,0:T(8,128)(2,1)S(1)}, bf16[5120,128]{1,0:T(8,128)(2,1)}, u32[]{:S(2)}) copy-start(bf16[5120,128]{1,0:T(8,128)(2,1)} %param.20) | copy-start | bytes 3932164
  11.6 19.3 %all-to-all-start.1 = ((bf16[16,4,2048]{2,1,0:T(4,128)(2,1)}), bf16[16,4,2048]{2,1,0:T(4,128)(2,1)S(1)}, u32[]{:S(2)}, u32[]{:S(2)}) async-start(bf16[16,4,2048]{2,1,0:T(4,128)(2,1)} %all_to_all.67), calls=%async_computation.1 | async-start | bytes 524288 | tf_op jit(solution)/shard_map/all_to_all | solution.py:211
  30.9 18.3 %all-to-all-start = ((bf16[16,4,2048]{2,1,0:T(4,128)(2,1)}), bf16[16,4,2048]{2,1,0:T(4,128)(2,1)S(1)}, u32[]{:S(2)}, u32[]{:S(2)}) async-start(bf16[16,4,2048]{2,1,0:T(4,128)(2,1)} %all_to_all.64), calls=%async_computation | async-start | bytes 524288 | tf_op jit(solution)/shard_map/all_to_all | solution.py:181
  49.2 29.4 %copy-start.8 = (bf16[16,4,2048]{2,1,0:T(4,128)(2,1)}, bf16[16,4,2048]{2,1,0:T(4,128)(2,1)S(1)}, u32[]{:S(2)}) copy-start(bf16[16,4,2048]{2,1,0:T(4,128)(2,1)S(1)} %all-to-all-done) | copy-start | bytes 786436
  49.2 24.1 %all-to-all-start.3 = ((bf16[16,4,5120]{2,1,0:T(4,128)(2,1)}), bf16[16,4,5120]{2,1,0:T(4,128)(2,1)S(1)}, u32[]{:S(2)}, u32[]{:S(2)}) async-start(bf16[16,4,5120]{2,1,0:T(4,128)(2,1)} %all_to_all.73), calls=%async_computation.3 | async-start | bytes 1310720 | tf_op jit(solution)/shard_map/all_to_all | solution.py:204
  73.3 36.9 %all-to-all-start.2 = ((bf16[16,4,5120]{2,1,0:T(4,128)(2,1)}), bf16[16,4,5120]{2,1,0:T(4,128)(2,1)S(1)}, u32[]{:S(2)}, u32[]{:S(2)}) async-start(bf16[16,4,5120]{2,1,0:T(4,128)(2,1)} %all_to_all.70), calls=%async_computation.2 | async-start | bytes 1310720 | tf_op jit(solution)/shard_map/all_to_all | solution.py:174
  102.0 8.2 %copy-start.13 = (s32[1,256]{1,0:T(1,128)S(1)}, s32[1,256]{1,0:T(1,128)}, u32[]{:S(2)}) copy-start(s32[1,256]{1,0:T(1,128)} %param.26) | copy-start | bytes 3076
  104.4 10.8 %copy-start.12 = (s32[1,256]{1,0:T(1,128)S(1)}, s32[1,256]{1,0:T(1,128)}, u32[]{:S(2)}) copy-start(s32[1,256]{1,0:T(1,128)} %param.27) | copy-start | bytes 3076
  105.5 9.9 %copy-start.14 = (s32[1,256]{1,0:T(1,128)S(1)}, s32[1,256]{1,0:T(1,128)}, u32[]{:S(2)}) copy-start(s32[1,256]{1,0:T(1,128)} %param.26) | copy-start | bytes 3076
  105.5 11.9 %copy-start.9 = (bf16[16,4,2048]{2,1,0:T(4,128)(2,1)S(1)}, bf16[16,4,2048]{2,1,0:T(4,128)(2,1)}, u32[]{:S(2)}) copy-start(bf16[16,4,2048]{2,1,0:T(4,128)(2,1)} %copy-done.8) | copy-start | bytes 786436
  110.2 7.2 %copy-start.4 = (bf16[16,4,5120]{2,1,0:T(4,128)(2,1)}, bf16[16,4,5120]{2,1,0:T(4,128)(2,1)S(1)}, u32[]{:S(2)}) copy-start(bf16[16,4,5120]{2,1,0:T(4,128)(2,1)S(1)} %all-to-all-done.2) | copy-start | bytes 1966084
  110.2 23.0 %all-to-all-start.5 = ((bf16[16,4,5120]{2,1,0:T(4,128)(2,1)}), bf16[16,4,5120]{2,1,0:T(4,128)(2,1)}, u32[]{:S(2)}, u32[]{:S(2)}) async-start(bf16[16,4,5120]{2,1,0:T(4,128)(2,1)} %all_to_all.79), calls=%async_computation.5 | async-start | bytes 1310720 | tf_op jit(solution)/shard_map/all_to_all | solution.py:218
  133.2 30.5 %all-to-all-start.4 = ((bf16[16,4,5120]{2,1,0:T(4,128)(2,1)}), bf16[16,4,5120]{2,1,0:T(4,128)(2,1)S(1)}, u32[]{:S(2)}, u32[]{:S(2)}) async-start(bf16[16,4,5120]{2,1,0:T(4,128)(2,1)} %all_to_all.76), calls=%async_computation.4 | async-start | bytes 1310720 | tf_op jit(solution)/shard_map/all_to_all | solution.py:188
  144.5 2.4 copy-start.5
  163.7 32.1 %all-to-all-start.7 = ((bf16[16,4,5120]{2,1,0:T(4,128)(2,1)}), bf16[16,4,5120]{2,1,0:T(4,128)(2,1)S(1)}, u32[]{:S(2)}, u32[]{:S(2)}) async-start(bf16[16,4,5120]{2,1,0:T(4,128)(2,1)} %all_to_all.85), calls=%async_computation.7 | async-start | bytes 1310720 | tf_op jit(solution)/shard_map/all_to_all | solution.py:197
  191.3 12.1 %copy-start.2 = (f32[8,256,128]{2,1,0:T(8,128)S(1)}, f32[8,256,128]{2,1,0:T(8,128)}, u32[]{:S(2)}) copy-start(f32[8,256,128]{2,1,0:T(8,128)} %custom-call.8) | copy-start | bytes 3145732
  195.7 7.6 %copy-start.3 = (bf16[16,4,5120]{2,1,0:T(4,128)(2,1)}, bf16[16,4,5120]{2,1,0:T(4,128)(2,1)S(1)}, u32[]{:S(2)}) copy-start(bf16[16,4,5120]{2,1,0:T(4,128)(2,1)S(1)} %all-to-all-done.7) | copy-start | bytes 1966084
  195.7 90.5 %all-to-all-start.6 = ((bf16[16,4,5120]{2,1,0:T(4,128)(2,1)}), bf16[16,4,5120]{2,1,0:T(4,128)(2,1)}, u32[]{:S(2)}, u32[]{:S(2)}) async-start(bf16[16,4,5120]{2,1,0:T(4,128)(2,1)} %all_to_all.82), calls=%async_computation.6 | async-start | bytes 1310720 | tf_op jit(solution)/shard_map/all_to_all | solution.py:167
  203.1 372.2 %all-reduce.5.cloned.1.call-start = ((), (), s32[]{:S(2)}) async-start(), calls=%async_computation.8 | async-start | bytes 6291456
  209.6 2.4 copy-start.16
  219.8 2.4 copy-start.16
  230.0 2.4 copy-start.16
  240.2 2.4 copy-start.16
  250.3 2.4 copy-start.16
  260.5 2.4 copy-start.16
  270.7 2.4 copy-start.16
  280.8 2.4 copy-start.16
  300.8 2.9 copy-start.6
  300.8 3.1 copy-start.10
  300.8 3.1 copy-start.11
  303.8 1.1 copy-start.15
  304.4 2.0 copy-start.1
  (1 other events, 1.0 us)
Sparse Core Ops, SparseCore 0:
  309.2 266.0 all-reduce.4
where the time goes:
time: 595 us; the launch traced here: 585 us
  waiting for transfers between devices  300 us (50%)
  local copies, waits for them, and re-layouts  115 us (19%)
  matrix products  57.8 us (10%)
  starting transfers between devices  55.4 us (9%)
  other arithmetic  27.3 us (5%)
  loops' own time  15.9 us (3%)
  between operations  14.7 us (2%)
    unnamed x2, waiting for transfers between devices  264 us
    scatter x8, local copies, waits for them, and re-layouts, pack_rows(): return empty_rows.at[slot_ids].set(source_rows, mode='drop')  39.4 us
    gather x4, local copies, waits for them, and re-layouts, assemble(): return jnp.take(arrivals, arrival_pick_index, axis=0)  28.8 us
    sub x8, matrix products, per_group(): weights = jnp.exp(scores - row_max)  19.8 us
    dot_general x8, matrix products, per_group(): jnp.einsum('sij,isd->jd', probs.astype(jnp.bfloat16), grad_block, preferr...  19.1 us
    another operation x1, loops' own time, attention_backward(): lax.map(per_group, jnp.arange(KV_HEADS, dtype=jnp.int32))  15.9 us
    all_to_all x1, waiting for transfers between devices, local(): lax.all_to_all(pack_rows(queries, node_slots, far_total), 'node', split_a...  11.9 us
  transfers between devices with their start and end apart: 9, of which 6 were waited for; matrix products, arithmetic and copies ran while one was open for 26% of the time, Pallas kernels for 0%

commit v1 on v0

v1 whole, which is shorter than its diff:
```python
import functools
import math

import numpy as np

import jax
import jax.numpy as jnp
from jax import lax
from jax.experimental import pallas as pl
from jax.experimental.pallas import tpu as pltpu
from jax.sharding import PartitionSpec as P

KV_HEADS = 8
HEAD = 128
ADAPTER_RANK = 64
CAP_L = 4
CAP_N = 4
GROUP = 5
KEY_HEAD_WIDTH = 1024
MODEL_WIDTH = 5120
ROWS = 256
PEERS = 16
MOVED = PEERS * CAP_L
ARRIVALS = ROWS + 2 * MOVED
ROPE_THETA = 1000000.0

QUARTERS = 4
GROUP_WIDTH = GROUP * HEAD
HEAD_COLS = 2 * GROUP_WIDTH + 2 * HEAD
HEAD_QUARTER = HEAD_COLS // QUARTERS
ATT_COLS = KV_HEADS * HEAD_QUARTER
X_QUARTER = MODEL_WIDTH // QUARTERS
LOG2E = math.log2(math.e)
BF = jnp.bfloat16
F32 = jnp.float32
MIB = 1 << 20
VMEM_LIMIT = 62 * MIB

DOWN_SHARD = 20
UP_SHARD = 4
SHARD = DOWN_SHARD + UP_SHARD
BLOCK_DEV = 32
BLOCK_COUNT = 8
DOWN_BLOCK = BLOCK_DEV * DOWN_SHARD
UP_BLOCK = BLOCK_DEV * UP_SHARD
BLOCK_ROWS = BLOCK_DEV * SHARD


def dot(a, b):
    return jnp.dot(a, b, preferred_element_type=F32)


def dot_nt(a, b):
    return lax.dot_general(a, b, (((1,), (1,)), ((), ())), preferred_element_type=F32)


def dot_tn(a, b):
    return lax.dot_general(a, b, (((0,), (0,)), ((), ())), preferred_element_type=F32)


def iota(shape, dim):
    return lax.broadcasted_iota(jnp.int32, shape, dim)


def interleave(rows, scratch):
    blocks = scratch.shape[0]
    for c in range(QUARTERS):
        for i in range(blocks):
            at = (c * blocks + i) * HEAD
            scratch[i, pl.ds(c, MOVED, stride=QUARTERS), :] = rows[:, at : at + HEAD]
    wide = jnp.concatenate([scratch[i] for i in range(blocks)], axis=1)
    return wide.astype(BF).reshape(PEERS, 16, blocks * HEAD)


def gather_quarters(rows, scratch):
    blocks = scratch.shape[0]
    wide = rows.reshape(ROWS, blocks * HEAD).astype(F32)
    for i in range(blocks):
        scratch[i] = wide[:, i * HEAD : (i + 1) * HEAD]
    return jnp.concatenate(
        [
            scratch[i, pl.ds(c, MOVED, stride=QUARTERS), :]
            for c in range(QUARTERS)
            for i in range(blocks)
        ],
        axis=1,
    ).astype(BF)


X_STEPS = 5
X_STEP = X_QUARTER // X_STEPS


def columns(j, width):
    return slice(j * width, (j + 1) * width)


def pack_kernel(near, target, q, g, kv, x, *rest):
    if near:
        att_out, *rest = rest
        x_out, x_from = att_out, ATT_COLS
    else:
        down, att_out, x_out, down_out, *rest = rest
        x_from = 0
    q_in, g_in, kv_in, x_in, att, att_x, spread, spread_x, head_sem, x_sem, out_sem, *rest = rest

    loads = [pltpu.make_async_copy(kv, kv_in, head_sem.at[2 * KV_HEADS])]
    for j in range(KV_HEADS):
        part = columns(j, GROUP_WIDTH)
        loads.append(pltpu.make_async_copy(q.at[:, part], q_in.at[:, part], head_sem.at[2 * j]))
        loads.append(
            pltpu.make_async_copy(g.at[:, part], g_in.at[:, part], head_sem.at[2 * j + 1])
        )
    x_loads = []
    for c in range(QUARTERS):
        part = columns(c, X_QUARTER)
        x_loads.append(pltpu.make_async_copy(x.at[:, part], x_in.at[:, part], x_sem.at[c]))
    if not near:
        down_in, att_down, down_sem = rest
        x_loads.append(pltpu.make_async_copy(down, down_in, down_sem.at[0]))
    for load in loads + x_loads:
        load.start()

    select = jnp.where(iota((MOVED, ROWS), 0) == target[...], 1.0, 0.0).astype(BF)
    stores = []

    def send(source, to, sem):
        stores.append(pltpu.make_async_copy(source, to, sem))
        stores[-1].start()

    loads[0].wait()
    for j in range(KV_HEADS):
        loads[1 + 2 * j].wait()
        loads[2 + 2 * j].wait()
        part = columns(j, GROUP_WIDTH)
        rows = jnp.concatenate(
            [
                q_in[:, part],
                g_in[:, part],
                kv_in[:, columns(j, HEAD)],
                kv_in[:, columns(KV_HEADS + j, HEAD)],
            ],
            axis=1,
        )
        part = columns(j, HEAD_QUARTER)
        att[:, :, part] = interleave(dot(select, rows), spread.at[j % 2])
        send(att.at[:, :, part], att_out.at[:, :, part], out_sem.at[j])
    for load in x_loads:
        load.wait()
    for j in range(X_STEPS):
        rows = jnp.concatenate(
            [x_in[:, columns(c * X_STEPS + j, X_STEP)] for c in range(QUARTERS)], axis=1
        )
        part = columns(j, X_STEP)
        att_x[:, :, part] = interleave(dot(select, rows), spread_x.at[j % 2])
        to = slice(x_from + part.start, x_from + part.stop)
        send(att_x.at[:, :, part], x_out.at[:, :, to], out_sem.at[KV_HEADS + j])
    if not near:
        own_out = dot(x_in[...], down_in[...]).astype(BF)
        down_out[...] = own_out
        picked = dot(select, own_out)
        rows = jnp.concatenate([picked] + [jnp.zeros_like(picked)] * (QUARTERS - 1), axis=1)
        att_down[...] = interleave(rows, spread_x.at[0, :1])
        send(att_down, x_out.at[:, :, X_QUARTER:], down_sem.at[1])
    for store in stores:
        store.wait()


def pack(target, queries, grads, kv, activations, down=None):
    near = down is None
    hbm, vmem = pl.BlockSpec(memory_space=pltpu.HBM), pl.BlockSpec(memory_space=pltpu.VMEM)
    scratch = [
        pltpu.VMEM((ROWS, KV_HEADS * GROUP_WIDTH), BF),
        pltpu.VMEM((ROWS, KV_HEADS * GROUP_WIDTH), BF),
        pltpu.VMEM((ROWS, 2 * KEY_HEAD_WIDTH), BF),
        pltpu.VMEM((ROWS, MODEL_WIDTH), BF),
        pltpu.VMEM((PEERS, 16, ATT_COLS), BF),
        pltpu.VMEM((PEERS, 16, X_QUARTER), BF),
        pltpu.VMEM((2, HEAD_QUARTER // HEAD, ROWS, HEAD), F32),
        pltpu.VMEM((2, X_STEP // HEAD, ROWS, HEAD), F32),
        pltpu.SemaphoreType.DMA((2 * KV_HEADS + 1,)),
        pltpu.SemaphoreType.DMA((QUARTERS,)),
        pltpu.SemaphoreType.DMA((KV_HEADS + X_STEPS,)),
    ]
    if near:
        args, out_specs = (), [hbm]
        out_shape = [jax.ShapeDtypeStruct((PEERS, 16, ATT_COLS + X_QUARTER), BF)]
    else:
        args, out_specs = (down,), [hbm, hbm, vmem]
        out_shape = [
            jax.ShapeDtypeStruct((PEERS, 16, ATT_COLS), BF),
            jax.ShapeDtypeStruct((PEERS, 16, X_QUARTER + HEAD), BF),
            jax.ShapeDtypeStruct((ROWS, HEAD), BF),
        ]
        scratch += [
            pltpu.VMEM((MODEL_WIDTH, HEAD), BF),
            pltpu.VMEM((PEERS, 16, HEAD), BF),
            pltpu.SemaphoreType.DMA((2,)),
        ]
    return pl.pallas_call(
        functools.partial(pack_kernel, near),
        in_specs=[vmem] + [hbm] * (4 + len(args)),
        out_specs=out_specs,
        out_shape=out_shape,
        scratch_shapes=scratch,
        compiler_params=pltpu.CompilerParams(vmem_limit_bytes=VMEM_LIMIT),
        cost_estimate=pl.CostEstimate(
            flops=2 * MOVED * ROWS * QUARTERS * (ATT_COLS + X_QUARTER),
            bytes_accessed=14 * MIB,
            transcendentals=0,
        ),
        name="pack_rows",
    )(target, queries, grads, kv, activations, *args)


def near_kernel(near, down, x_out, down_out, spread):
    rows = gather_quarters(near[...], spread)
    x_out[...] = rows
    down_out[...] = dot(rows, down[...]).astype(BF)


def near_adapter_rows(near, down):
    return pl.pallas_call(
        near_kernel,
        grid=(1,),
        in_specs=[
            pl.BlockSpec((PEERS, 16, X_QUARTER), lambda i: (0, 0, 0)),
            pl.BlockSpec((MODEL_WIDTH, HEAD), lambda i: (0, 0)),
        ],
        out_specs=[
            pl.BlockSpec((MOVED, MODEL_WIDTH), lambda i: (0, 0)),
            pl.BlockSpec((MOVED, HEAD), lambda i: (0, 0)),
        ],
        out_shape=[
            jax.ShapeDtypeStruct((MOVED, MODEL_WIDTH), BF),
            jax.ShapeDtypeStruct((MOVED, HEAD), BF),
        ],
        scratch_shapes=[pltpu.VMEM((X_QUARTER // HEAD, ROWS, HEAD), F32)],
        compiler_params=pltpu.CompilerParams(vmem_limit_bytes=VMEM_LIMIT),
        cost_estimate=pl.CostEstimate(
            flops=2 * MOVED * MODEL_WIDTH * HEAD, bytes_accessed=3 * MIB, transcendentals=0
        ),
        name="near_adapter_rows",
    )(near, down)


def arrival_pick(pick, entry):
    return jnp.where(pick == entry, 1.0, 0.0).astype(BF)


def attention_kernel(
    pick_col, seg_row, seg_col, cos, sin, up, q, g, k, v, near, far, grad_out, lift_out,
    gather, bias, lift, spread, spread_far
):
    step = pl.program_id(0)

    @pl.when(step == 0)
    def _():
        gather[...] = arrival_pick(pick_col[...], iota((ROWS, ARRIVALS), 1))
        allowed = (seg_col[...] == seg_row[...]) & (
            iota((ROWS, ROWS), 0) <= iota((ROWS, ROWS), 1)
        )
        bias[...] = jnp.where(allowed, 0.0, -1e30)
        lift[...] = jnp.zeros_like(lift)

    columns = jnp.concatenate([q[...], g[...], k[...], v[...]], axis=1)
    near_rows = gather_quarters(near[...], spread)
    far_rows = gather_quarters(far[...], spread_far)
    packed = dot(gather[...], jnp.concatenate([columns, near_rows, far_rows], axis=0)).astype(BF)
    key = packed[:, 2 * GROUP_WIDTH : 2 * GROUP_WIDTH + HEAD]
    value = packed[:, 2 * GROUP_WIDTH + HEAD :]
    score_scale = 1.0 / math.sqrt(HEAD)

    half = ROWS // 2
    sums = []
    for block in range(2):
        rows = slice(block * half, (block + 1) * half)
        keys = (block + 1) * half
        query = jnp.concatenate(
            [packed[rows, h * HEAD : (h + 1) * HEAD] for h in range(GROUP)], axis=0
        )
        grad = jnp.concatenate(
            [packed[rows, GROUP_WIDTH + h * HEAD : GROUP_WIDTH + (h + 1) * HEAD] for h in range(GROUP)],
            axis=0,
        )
        block_bias = jnp.concatenate([bias[:keys, rows]] * GROUP, axis=1)
        scores = dot_nt(key[:keys], query) * (score_scale * LOG2E) + block_bias
        weights = jnp.exp2(scores - jnp.max(scores, axis=0, keepdims=True))
        probs = weights * (1.0 / jnp.sum(weights, axis=0, keepdims=True))
        prob_grad = dot_nt(value[:keys], grad)
        delta = jnp.sum(probs * prob_grad, axis=0, keepdims=True)
        score_grad = (probs * (prob_grad - delta)).astype(BF)
        sums.append((dot(score_grad, query), dot(probs.astype(BF), grad)))
    key_rot = jnp.concatenate([sums[0][0] + sums[1][0][:half], sums[1][0][half:]], axis=0)
    value_grad = jnp.concatenate([sums[0][1] + sums[1][1][:half], sums[1][1][half:]], axis=0)
    key_rot = key_rot * score_scale
    swapped = jnp.concatenate([key_rot[:, HEAD // 2 :], key_rot[:, : HEAD // 2]], axis=1)
    key_grad = key_rot * cos[...] + swapped * sin[...]

    key_grad = key_grad.astype(BF)
    value_grad = value_grad.astype(BF)
    grad_out[:, pl.ds(pl.multiple_of(step * HEAD, HEAD), HEAD)] = key_grad
    grad_out[:, pl.ds(pl.multiple_of(KEY_HEAD_WIDTH + step * HEAD, HEAD), HEAD)] = value_grad
    up_rows = up[...]
    zero = jnp.zeros((ADAPTER_RANK, HEAD), BF)
    key_up = jnp.concatenate([up_rows[:ADAPTER_RANK], zero], axis=0)
    value_up = jnp.concatenate([zero, up_rows[ADAPTER_RANK:]], axis=0)
    lift[...] += dot_nt(
        jnp.concatenate([key_grad, value_grad], axis=1),
        jnp.concatenate([key_up, value_up], axis=1),
    )

    @pl.when(step == KV_HEADS - 1)
    def _():
        lift_out[...] = lift[...].astype(BF)


def attention(pick_col, seg_row, seg_col, cos, sin, up, queries, grads, kv, near, far):
    def whole(shape):
        return pl.BlockSpec(shape, lambda j: (0,) * len(shape))

    def head_block(width):
        return pl.BlockSpec((ROWS, width), lambda j: (0, j))

    arrived = pl.BlockSpec((PEERS, 16, HEAD_QUARTER), lambda j: (0, 0, j))
    return pl.pallas_call(
        attention_kernel,
        grid=(KV_HEADS,),
        in_specs=[
            whole((ROWS, 1)),
            whole((1, ROWS)),
            whole((ROWS, 1)),
            whole((ROWS, HEAD)),
            whole((ROWS, HEAD)),
            pl.BlockSpec((2 * ADAPTER_RANK, HEAD), lambda j: (0, j)),
            head_block(GROUP_WIDTH),
            head_block(GROUP_WIDTH),
            head_block(HEAD),
            pl.BlockSpec((ROWS, HEAD), lambda j: (0, KV_HEADS + j)),
            arrived,
            arrived,
        ],
        out_specs=[whole((ROWS, 2 * KEY_HEAD_WIDTH)), whole((ROWS, HEAD))],
        out_shape=[
            jax.ShapeDtypeStruct((ROWS, 2 * KEY_HEAD_WIDTH), BF),
            jax.ShapeDtypeStruct((ROWS, HEAD), BF),
        ],
        scratch_shapes=[
            pltpu.VMEM((ROWS, ARRIVALS), BF),
            pltpu.VMEM((ROWS, ROWS), F32),
            pltpu.VMEM((ROWS, HEAD), F32),
            pltpu.VMEM((HEAD_QUARTER // HEAD, ROWS, HEAD), F32),
            pltpu.VMEM((HEAD_QUARTER // HEAD, ROWS, HEAD), F32),
        ],
        compiler_params=pltpu.CompilerParams(vmem_limit_bytes=VMEM_LIMIT),
        cost_estimate=pl.CostEstimate(
            flops=12 * 10**9, bytes_accessed=14 * MIB, transcendentals=2 * 10**6
        ),
        name="attention_grads",
    )(pick_col, seg_row, seg_col, cos, sin, up, queries, grads, kv, kv, near, far)


def adapter_kernel(
    pick_row, pick_col, order_col, lift, own_down, near_down, near_x, far, x, kv_grad, out,
    x_in, kv_in, far_in, near_in, placed_out, spread, load_sem, out_sem
):
    loads = [
        pltpu.make_async_copy(far, far_in, load_sem.at[0]),
        pltpu.make_async_copy(kv_grad, kv_in, load_sem.at[1]),
        pltpu.make_async_copy(near_x, near_in, load_sem.at[2]),
    ]
    for c in range(QUARTERS):
        part = columns(c, X_QUARTER)
        loads.append(pltpu.make_async_copy(x.at[:, part], x_in.at[:, part], load_sem.at[3 + c]))
    for load in loads:
        load.start()

    order = jnp.where(iota((BLOCK_ROWS, BLOCK_ROWS), 1) == order_col[...], 1.0, 0.0).astype(BF)
    gather = arrival_pick(pick_col[...], iota((ROWS, ARRIVALS), 1))
    spread_lift = arrival_pick(pick_row[...], iota((ARRIVALS, ROWS), 0))
    lifted = dot(spread_lift, lift[...]).astype(BF)

    loads[0].wait()
    far_rows = gather_quarters(far_in[:, :, :X_QUARTER], spread)
    spread[0] = far_in[:, :, X_QUARTER:].reshape(ROWS, HEAD).astype(F32)
    far_down = spread[0, pl.ds(0, MOVED, stride=QUARTERS), :].astype(BF)

    arrived_down = jnp.concatenate([own_down[...], near_down[...], far_down], axis=0)
    down_out = dot(gather, arrived_down).astype(BF)
    loads[1].wait()
    up_both = dot_tn(down_out, kv_in[...])
    up_sum = jnp.concatenate(
        [up_both[:ADAPTER_RANK, :KEY_HEAD_WIDTH], up_both[ADAPTER_RANK:, KEY_HEAD_WIDTH:]], axis=0
    ).astype(BF)

    loads[2].wait()
    stores = []
    for z_lo in range(BLOCK_COUNT // 2):
        part = columns(z_lo, X_QUARTER)
        loads[3 + z_lo].wait()
        arrived = jnp.concatenate([x_in[:, part], near_in[:, part], far_rows[:, part]], axis=0)
        down_sum = dot_tn(lifted, arrived).astype(BF)
        both = jnp.concatenate(
            [
                jnp.concatenate(
                    [
                        down_sum[:, columns(y_high, DOWN_BLOCK)],
                        up_sum[:, columns(2 * z_lo + y_high, UP_BLOCK)],
                    ],
                    axis=1,
                )
                for y_high in range(2)
            ],
            axis=0,
        )
        placed = dot_nt(order, both).astype(BF)
        rows = columns(z_lo, 2 * SHARD)
        for y_high in range(2):
            for c in range(2):
                for xx in range(4):
                    for y_low in range(2):
                        at = ((c * 4 + xx) * 2 + y_low) * 2 * SHARD
                        placed_out[c, xx * 4 + y_high * 2 + y_low, rows, :] = placed[
                            at : at + 2 * SHARD, columns(y_high, HEAD)
                        ]
        stores.append(
            pltpu.make_async_copy(
                placed_out.at[:, :, rows], out.at[:, :, rows], out_sem.at[z_lo]
            )
        )
        stores[-1].start()
    for store in stores:
        store.wait()


def shard_order():
    order = []
    for c in range(2):
        for xx in range(4):
            for y_low in range(2):
                for z_hi in range(2):
                    device = ((y_low * 4 + xx) * 2 + z_hi) * 2 + c
                    for r in range(DOWN_SHARD):
                        order.append(device * DOWN_SHARD + r)
                    for r in range(UP_SHARD):
                        order.append(DOWN_BLOCK + device * UP_SHARD + r)
    return np.asarray(order, np.int32).reshape(BLOCK_ROWS, 1)


def adapters(pick_row, pick_col, lift, own_down, near_down, near_x, far, x, kv_grad):
    hbm, vmem = pl.BlockSpec(memory_space=pltpu.HBM), pl.BlockSpec(memory_space=pltpu.VMEM)
    order_col = jnp.asarray(shard_order())
    return pl.pallas_call(
        adapter_kernel,
        out_shape=jax.ShapeDtypeStruct((2, 16, 8 * SHARD, HEAD), BF),
        in_specs=[vmem] * 6 + [hbm] * 4,
        out_specs=hbm,
        scratch_shapes=[
            pltpu.VMEM((ROWS, MODEL_WIDTH), BF),
            pltpu.VMEM((ROWS, 2 * KEY_HEAD_WIDTH), BF),
            pltpu.VMEM((PEERS, 16, X_QUARTER + HEAD), BF),
            pltpu.VMEM((MOVED, MODEL_WIDTH), BF),
            pltpu.VMEM((2, 16, 8 * SHARD, HEAD), BF),
            pltpu.VMEM((X_QUARTER // HEAD, ROWS, HEAD), F32),
            pltpu.SemaphoreType.DMA((3 + QUARTERS,)),
            pltpu.SemaphoreType.DMA((BLOCK_COUNT // 2,)),
        ],
        compiler_params=pltpu.CompilerParams(vmem_limit_bytes=VMEM_LIMIT),
        cost_estimate=pl.CostEstimate(
            flops=4 * 10**9, bytes_accessed=10 * MIB, transcendentals=0
        ),
        name="adapter_grads",
    )(pick_row, pick_col, order_col, lift, own_down, near_down, near_x, far, x, kv_grad)


def device_groups(axes):
    names = ["z_lo", "y", "x", "z_hi", "core"]
    index = np.arange(256).reshape(4, 4, 4, 2, 2)
    moved = [names.index(a) for a in axes]
    rest = [i for i in range(5) if i not in moved]
    size = math.prod(index.shape[i] for i in moved)
    return index.transpose(rest + moved).reshape(-1, size).tolist()


def exchange(array, axes):
    return lax.all_to_all(
        array,
        ("node", "local"),
        split_axis=0,
        concat_axis=0,
        axis_index_groups=device_groups(axes),
        tiled=True,
    )


def sum_over_devices(parts):
    both = exchange(parts, ["core"])
    total = (both[0].astype(F32) + both[1].astype(F32)).astype(BF)
    total = jnp.sum(exchange(total, ["x", "y"]).astype(F32), axis=0)
    total = total.reshape(8, SHARD, HEAD)
    return jnp.sum(exchange(total, ["z_lo", "z_hi"]), axis=0)


def rope_tables(segments):
    slot_ids = jnp.arange(segments.shape[0], dtype=jnp.int32)
    seg_start = jnp.sum((segments[None, :] < segments[:, None]).astype(jnp.int32), axis=1)
    position = (slot_ids - seg_start).astype(F32)
    frequency = ROPE_THETA ** (-jnp.arange(0, HEAD, 2).astype(F32) / HEAD)
    angles = position[:, None] * frequency[None, :]
    cosine, sine = jnp.cos(angles), jnp.sin(angles)
    return (
        jnp.concatenate([cosine, cosine], axis=1),
        jnp.concatenate([sine, -sine], axis=1),
    )


def local(
    activations,
    queries,
    rotated_key_value,
    attention_out_grad,
    adapter_down,
    adapter_up,
    bin_local_index,
    bin_row_offset,
    spill_node,
    spill_row_offset,
    arrival_pick_index,
    packed_sequence_number,
):
    own_local = lax.axis_index("local")
    own_node = lax.axis_index("node")
    moved_in = bin_local_index != own_local
    moved_out = jnp.logical_not(moved_in) & (spill_node != own_node)
    near_target = jnp.where(moved_in, bin_local_index * CAP_L + bin_row_offset, -1)
    far_target = jnp.where(moved_out, spill_node * CAP_N + spill_row_offset, -1)

    rows = (queries, attention_out_grad, rotated_key_value, activations)
    (near_send,) = pack(near_target, *rows)
    far_send, far_x_send, own_down = pack(far_target, *rows, adapter_down)

    near = lax.all_to_all(near_send, "local", split_axis=0, concat_axis=0, tiled=True)
    far_send, near = lax.optimization_barrier((far_send, near))
    far = lax.all_to_all(far_send, "node", split_axis=0, concat_axis=0, tiled=True)
    near_x, near_down = near_adapter_rows(near[:, :, ATT_COLS:], adapter_down)
    pick_row = arrival_pick_index
    pick_col = arrival_pick_index.reshape(ROWS, 1)
    seg_row = packed_sequence_number
    seg_col = packed_sequence_number.reshape(ROWS, 1)
    cos, sin = rope_tables(packed_sequence_number.reshape(-1))
    far_x_send, far, near_x, near_down, pick_col, seg_col, cos, sin = lax.optimization_barrier(
        (far_x_send, far, near_x, near_down, pick_col, seg_col, cos, sin)
    )
    far_x = lax.all_to_all(far_x_send, "node", split_axis=0, concat_axis=0, tiled=True)

    kv_grad, lift = attention(
        pick_col,
        seg_row,
        seg_col,
        cos,
        sin,
        adapter_up,
        queries,
        attention_out_grad,
        rotated_key_value,
        near,
        far,
    )
    parts = adapters(
        pick_row,
        pick_col,
        lift,
        own_down,
        near_down,
        near_x,
        far_x,
        activations,
        kv_grad,
    )
    total = sum_over_devices(parts) * (1.0 / math.sqrt(256 * ROWS))
    return (kv_grad, total[:DOWN_SHARD], total[DOWN_SHARD:])


def solution(mesh):
    split = P(("node", "local"), None)
    return jax.shard_map(
        local,
        mesh=mesh,
        in_specs=(split,) * 4 + (P(), P()) + (split,) * 6,
        out_specs=(split,) * 3,
        check_vma=False,
    )
```

time: 595 us -> 189 us (0.32); the launches traced: 585 us -> 188 us
  waiting for transfers between devices: 300 us -> 54.6 us
  local copies, waits for them, and re-layouts: 115 us -> 4.15 us
  matrix products: 57.8 us -> 0 us
  Pallas kernels: 0 us -> 42 us
  blocking collectives: 0 us -> 38.1 us
  other arithmetic: 27.3 us -> 3.2 us
  loops' own time: 15.9 us -> 0 us
  between operations: 14.7 us -> 0.75 us
  starting transfers between devices: 55.4 us -> 45 us
    unnamed x2 -> x0, waiting for transfers between devices: 264 us -> none
    pallas_call x0 -> x5, Pallas kernels: none -> 42 us  [the longest x1 16.8 us: attention(): pl.pallas_call(attention_kernel, grid=(KV_HEADS,), in_specs=[whole((ROWS,...]
    scatter x8 -> x0, local copies, waits for them, and re-layouts: 39.4 us -> none  [pack_rows(): return empty_rows.at[slot_ids].set(source_rows, mode='drop')]
    all_to_all x0 -> x3, blocking collectives: none -> 38.1 us  [exchange(): lax.all_to_all(array, ('node', 'local'), split_axis=0, concat_axis=0, axi...]
    dot_general x30 -> x0, matrix products: 38 us -> none  [the longest x8 19.1 us: per_group(): jnp.einsum('sij,isd->jd', probs.astype(jnp.bfloat16), grad_block, preferr...]
    gather x4 -> x0, local copies, waits for them, and re-layouts: 28.8 us -> none  [assemble(): return jnp.take(arrivals, arrival_pick_index, axis=0)]
    all_to_all x16 -> x0, local copies, waits for them, and re-layouts: 20.9 us -> none  [the longest x2 4.58 us: local(): lax.all_to_all(pack_rows(activations, local_slots, near_total), 'local',...]
    sub x8 -> x0, matrix products: 19.8 us -> none  [per_group(): weights = jnp.exp(scores - row_max)]
  transfers between devices with their start and end apart: 9 -> 3, of which waited for: 6 -> 2; matrix products, arithmetic and copies ran while one was open for 26% -> 3% of each run, Pallas kernels for 0% -> 15%
where the time goes in v1:
time: 189 us; the launch traced here: 188 us
  waiting for transfers between devices  54.6 us (29%)
  starting transfers between devices  45 us (24%)
  Pallas kernels  42 us (22%)
  blocking collectives  38.1 us (20%)
  local copies, waits for them, and re-layouts  4.15 us (2%)
  other arithmetic  3.2 us (2%)
    all_to_all x3, blocking collectives, exchange(): lax.all_to_all(array, ('node', 'local'), split_axis=0, concat_axis=0, axi...  38.1 us
    all_to_all x1, waiting for transfers between devices, local(): lax.all_to_all(near_send, 'local', split_axis=0, concat_axis=0, tiled=True)  27.4 us
    all_to_all x1, waiting for transfers between devices, local(): lax.all_to_all(far_send, 'node', split_axis=0, concat_axis=0, tiled=True)  27.2 us
    all_to_all x1, starting transfers between devices, local(): lax.all_to_all(far_send, 'node', split_axis=0, concat_axis=0, tiled=True)  25.2 us
    pallas_call x1, Pallas kernels, attention(): pl.pallas_call(attention_kernel, grid=(KV_HEADS,), in_specs=[whole((ROWS,...  16.8 us
    pallas_call x2, Pallas kernels, pack(): pl.pallas_call(functools.partial(pack_kernel, near), in_specs=[vmem] + [h...  14.4 us
    all_to_all x1, starting transfers between devices, local(): lax.all_to_all(near_send, 'local', split_axis=0, concat_axis=0, tiled=True)  11.5 us
    all_to_all x1, starting transfers between devices, local(): lax.all_to_all(far_x_send, 'node', split_axis=0, concat_axis=0, tiled=True)  8.3 us
  transfers between devices with their start and end apart: 3, of which 2 were waited for; matrix products, arithmetic and copies ran while one was open for 3% of the time, Pallas kernels for 15%

profile of v1, /device:TPU:2, one launch (start us, length us, event | category | flops | bytes accessed | tf_op | source)
XLA Modules:
  0.0 187.8 jit_solution(3163095407656670141)
XLA Ops:
  0.6 1.3 compare_select_fusion
  1.9 6.2 %pack_rows.3 = bf16[16,16,4352]{2,1,0:T(8,128)(2,1)} custom-call(s32[1,256]{1,0:T(1,128)} %get-tuple-element.40.target, bf16[256,5120]{1,0:T(8,128)(2,1)} %q.5, bf16[256,5120]{1,0:T(8,128)(2,1)} %g.5, bf16[256,2048]{1,0:T(8,128)(2,1)} %v.1, bf16[256,5120]{1,0:T(8,128)(2,1)} %x.5), custom_call_target="tpu_custom_call" | custom-call | flops 570425344 | bytes 14680064 | tf_op jit(solution)/shard_map/pack_rows/pallas_call | solution.py:200
  8.1 11.5 %all-to-all-start = ((bf16[16,16,4352]{2,1,0:T(8,128)(2,1)}), bf16[16,16,4352]{2,1,0:T(8,128)(2,1)}, u32[]{:S(2)}, u32[]{:S(2)}) async-start(bf16[16,16,4352]{2,1,0:T(8,128)(2,1)} %pack_rows.3), calls=%async_computation | async-start | bytes 4456448 | tf_op jit(solution)/shard_map/all_to_all | solution.py:542
  19.6 8.2 %pack_rows.2 = (bf16[16,16,3072]{2,1,0:T(8,128)(2,1)}, bf16[16,16,1408]{2,1,0:T(8,128)(2,1)}, bf16[256,128]{1,0:T(8,128)(2,1)}) custom-call(s32[1,256]{1,0:T(1,128)} %get-tuple-element.41.target, bf16[256,5120]{1,0:T(8,128)(2,1)} %q.5, bf16[256,5120]{1,0:T(8,128)(2,1)} %g.5, bf16[256,2048]{1,0:T(8,128)(2,1)} %v.1, bf16[256,5120]{1,0:T(8,128)(2,1)} %x.5, ...), custom_call_target="tpu_custom_call" | custom-call | flops 570425344 | bytes 14680064 | tf_op jit(solution)/shard_map/pack_rows/pallas_call | solution.py:200
  27.8 27.4 %all-to-all-done.near = bf16[16,16,4352]{2,1,0:T(8,128)(2,1)} async-done(((bf16[16,16,4352]{2,1,0:T(8,128)(2,1)}), bf16[16,16,4352]{2,1,0:T(8,128)(2,1)}, u32[]{:S(2)}, u32[]{:S(2)}) %all-to-all-start) | async-done | bytes 2228256 | tf_op jit(solution)/shard_map/all_to_all | solution.py:542
  55.2 0.0 copy-start.2
  55.2 25.2 %all-to-all-start.1 = ((bf16[16,16,3072]{2,1,0:T(8,128)(2,1)}), bf16[16,16,3072]{2,1,0:T(8,128)(2,1)S(1)}, u32[]{:S(2)}, u32[]{:S(2)}) async-start(bf16[16,16,3072]{2,1,0:T(8,128)(2,1)} %get-tuple-element.22), calls=%async_computation.1 | async-start | bytes 3145728 | tf_op jit(solution)/shard_map/all_to_all | solution.py:544
  80.4 0.0 copy-done.2
  80.4 0.2 convert_reduce_fusion.1
  80.6 0.5 multiply_sine_fusion
  81.2 0.8 pad_maximum_fusion
  82.0 2.0 %slice.15.near = bf16[16,16,1280]{2,1,0:T(8,128)(2,1)} slice(bf16[16,16,4352]{2,1,0:T(8,128)(2,1)} %all-to-all-done.near), slice={[0:16], [0:16], [3072:4352]} | slice | bytes 1310720 | tf_op jit(solution)/shard_map/slice | solution.py:545
  84.0 0.0 copy-start.3
  84.0 2.7 %near_adapter_rows.1 = (bf16[64,5120]{1,0:T(8,128)(2,1)}, bf16[64,128]{1,0:T(8,128)(2,1)}) custom-call(bf16[16,16,1280]{2,1,0:T(8,128)(2,1)} %slice.15.near, bf16[5120,128]{1,0:T(8,128)(2,1)} %down.1), custom_call_target="tpu_custom_call" | custom-call | flops 83886080 | bytes 3145728 | tf_op jit(solution)/shard_map/near_adapter_rows/pallas_call | solution.py:223
  86.6 27.2 %all-to-all-done.1.far = bf16[16,16,3072]{2,1,0:T(8,128)(2,1)S(1)} async-done(((bf16[16,16,3072]{2,1,0:T(8,128)(2,1)}), bf16[16,16,3072]{2,1,0:T(8,128)(2,1)S(1)}, u32[]{:S(2)}, u32[]{:S(2)}) %all-to-all-start.1) | async-done | bytes 1572896 | tf_op jit(solution)/shard_map/all_to_all | solution.py:544
  113.9 0.0 copy-start
  113.9 8.3 %all-to-all-start.2 = ((bf16[16,16,1408]{2,1,0:T(8,128)(2,1)}), bf16[16,16,1408]{2,1,0:T(8,128)(2,1)}, u32[]{:S(2)}, u32[]{:S(2)}) async-start(bf16[16,16,1408]{2,1,0:T(8,128)(2,1)} %get-tuple-element.36), calls=%async_computation.2 | async-start | bytes 1441792 | tf_op jit(solution)/shard_map/all_to_all | solution.py:554
  122.2 0.0 copy-done.3
  122.2 0.8 copy.19.pick_col
  123.0 0.8 copy.20.seg_col
  123.8 0.0 copy-done
  123.8 16.8 %attention_grads.1 = (bf16[256,2048]{1,0:T(8,128)(2,1)}, bf16[256,128]{1,0:T(8,128)(2,1)}) custom-call(s32[256,1]{1,0:T(8,128)} %copy.19.pick_col, s32[1,256]{1,0:T(1,128)} %seg_row.1, s32[256,1]{1,0:T(8,128)} %copy.20.seg_col, f32[256,128]{1,0:T(8,128)} %get-tuple-element.28.cos, f32[256,128]{1,0:T(8,128)} %get-tuple-element.29.sin, bf16[128,1024]{1,0:T(8,128)(2,1)} %up.1, ...), custom_call_target="tpu_custom_call" | custom-call | flops 12000000000 | bytes 14680064 | tf_op jit(solution)/shard_map/attention_grads/pallas_call | solution.py:326
  140.6 0.0 all-to-all-done.2.far
  140.6 8.2 %adapter_grads.1 = bf16[2,16,192,128]{3,2,1,0:T(8,128)(2,1)} custom-call(s32[1,256]{1,0:T(1,128)} %pick_row.1, s32[256,1]{1,0:T(8,128)} %copy.19.pick_col, s32[768,1]{1,0:T(8,128)} %constant.26.clone.order_col, bf16[256,128]{1,0:T(8,128)(2,1)} %get-tuple-element.32.lift, bf16[256,128]{1,0:T(8,128)(2,1)} %get-tuple-element.33.own_down, ...), custom_call_target="tpu_custom_call" | custom-call | flops 4000000000 | bytes 10485760 | tf_op jit(solution)/shard_map/adapter_grads/pallas_call | solution.py:453
  148.8 6.2 %all_to_all.30 = bf16[2,16,192,128]{3,2,1,0:T(8,128)(2,1)S(1)} all-to-all(bf16[2,16,192,128]{3,2,1,0:T(8,128)(2,1)} %adapter_grads.1), channel_id=1, replica_groups={{0,1},{2,3},{4,5},{6,7},{8,9},{10,11},{12,13},{14,15},{16,17},{18,19},{..., dimensions={0} | all-to-all | bytes 3145728 | tf_op jit(solution)/shard_map/all_to_all | solution.py:486
  154.9 0.2 fusion
  155.1 19.8 %all_to_all.31 = bf16[16,192,128]{2,1,0:T(8,128)(2,1)S(1)} all-to-all(bf16[16,192,128]{2,1,0:T(8,128)(2,1)S(1)} %fusion), channel_id=1, replica_groups={{0,16,32,48,4,20,36,52,8,24,40,56,12,28,44,60},{1,17,33,49,5,21,37,53,9..., dimensions={0} | all-to-all | bytes 1572864 | tf_op jit(solution)/shard_map/all_to_all | solution.py:486
  175.0 0.1 convert_reduce_fusion
  175.1 12.1 %all_to_all.32 = f32[8,24,128]{2,1,0:T(8,128)S(1)} all-to-all(f32[8,24,128]{2,1,0:T(8,128)S(1)} %bitcast.7), channel_id=1, replica_groups={{0,2,64,66,128,130,192,194},{1,3,65,67,129,131,193,195},{4,6,68,70,132,..., dimensions={0} | all-to-all | bytes 196608 | tf_op jit(solution)/shard_map/all_to_all | solution.py:486
  187.2 0.0 copy-start.1
  187.3 0.6 slice.23
  187.8 0.0 copy-done.1
  (4 shorter events, 0.0 us)
Async XLA Ops:
  8.1 47.0 %all-to-all-start = ((bf16[16,16,4352]{2,1,0:T(8,128)(2,1)}), bf16[16,16,4352]{2,1,0:T(8,128)(2,1)}, u32[]{:S(2)}, u32[]{:S(2)}) async-start(bf16[16,16,4352]{2,1,0:T(8,128)(2,1)} %pack_rows.3), calls=%async_computation | async-start | bytes 4456448 | tf_op jit(solution)/shard_map/all_to_all | solution.py:542
  55.2 25.2 %copy-start.2 = (s32[1,256]{1,0:T(1,128)S(1)}, s32[1,256]{1,0:T(1,128)}, u32[]{:S(2)}) copy-start(s32[1,256]{1,0:T(1,128)} %seg_row.1) | copy-start | bytes 3076
  55.2 58.7 %all-to-all-start.1 = ((bf16[16,16,3072]{2,1,0:T(8,128)(2,1)}), bf16[16,16,3072]{2,1,0:T(8,128)(2,1)S(1)}, u32[]{:S(2)}, u32[]{:S(2)}) async-start(bf16[16,16,3072]{2,1,0:T(8,128)(2,1)} %get-tuple-element.22), calls=%async_computation.1 | async-start | bytes 3145728 | tf_op jit(solution)/shard_map/all_to_all | solution.py:544
  84.0 38.3 %copy-start.3 = (s32[1,256]{1,0:T(1,128)S(1)}, s32[1,256]{1,0:T(1,128)}, u32[]{:S(2)}) copy-start(s32[1,256]{1,0:T(1,128)} %pick_row.1) | copy-start | bytes 3076
  113.9 9.9 %copy-start = (bf16[16,16,3072]{2,1,0:T(8,128)(2,1)}, bf16[16,16,3072]{2,1,0:T(8,128)(2,1)S(1)}, u32[]{:S(2)}) copy-start(bf16[16,16,3072]{2,1,0:T(8,128)(2,1)S(1)} %all-to-all-done.1.far) | copy-start | bytes 4718596
  113.9 26.7 %all-to-all-start.2 = ((bf16[16,16,1408]{2,1,0:T(8,128)(2,1)}), bf16[16,16,1408]{2,1,0:T(8,128)(2,1)}, u32[]{:S(2)}, u32[]{:S(2)}) async-start(bf16[16,16,1408]{2,1,0:T(8,128)(2,1)} %get-tuple-element.36), calls=%async_computation.2 | async-start | bytes 1441792 | tf_op jit(solution)/shard_map/all_to_all | solution.py:554
  187.2 0.6 copy-start.1

commit v2 on v1

--- a/solution.py
+++ b/solution.py
@@ -43,7 +43,10 @@
 BLOCK_COUNT = 8
 DOWN_BLOCK = BLOCK_DEV * DOWN_SHARD
 UP_BLOCK = BLOCK_DEV * UP_SHARD
-BLOCK_ROWS = BLOCK_DEV * SHARD
+PARTS = 4
+PART_ROWS = 4 * SHARD
+PART_COLS = 3 * HEAD
+PART_SHIFT = 32
 
 
 def dot(a, b):
@@ -95,7 +98,7 @@
     return slice(j * width, (j + 1) * width)
 
 
-def pack_kernel(near, target, q, g, kv, x, *rest):
+def pack_kernel(near, bin_local, bin_offset, spill_node, spill_offset, q, g, kv, x, *rest):
     if near:
         att_out, *rest = rest
         x_out, x_from = att_out, ATT_COLS
@@ -121,7 +124,13 @@
     for load in loads + x_loads:
         load.start()
 
-    select = jnp.where(iota((MOVED, ROWS), 0) == target[...], 1.0, 0.0).astype(BF)
+    stays_in = bin_local[...] == lax.axis_index("local")
+    if near:
+        target = jnp.where(stays_in, -1, bin_local[...] * CAP_L + bin_offset[...])
+    else:
+        moves = stays_in & (spill_node[...] != lax.axis_index("node"))
+        target = jnp.where(moves, spill_node[...] * CAP_N + spill_offset[...], -1)
+    select = jnp.where(iota((MOVED, ROWS), 0) == target, 1.0, 0.0).astype(BF)
     stores = []
 
     def send(source, to, sem):
@@ -166,7 +175,7 @@
         store.wait()
 
 
-def pack(target, queries, grads, kv, activations, down=None):
+def pack(plan, queries, grads, kv, activations, down=None):
     near = down is None
     hbm, vmem = pl.BlockSpec(memory_space=pltpu.HBM), pl.BlockSpec(memory_space=pltpu.VMEM)
     scratch = [
@@ -199,7 +208,7 @@
         ]
     return pl.pallas_call(
         functools.partial(pack_kernel, near),
-        in_specs=[vmem] + [hbm] * (4 + len(args)),
+        in_specs=[vmem] * 4 + [hbm] * (4 + len(args)),
         out_specs=out_specs,
         out_shape=out_shape,
         scratch_shapes=scratch,
@@ -210,7 +219,7 @@
             transcendentals=0,
         ),
         name="pack_rows",
-    )(target, queries, grads, kv, activations, *args)
+    )(*plan, queries, grads, kv, activations, *args)
 
 
 def near_kernel(near, down, x_out, down_out, spread):
@@ -244,29 +253,26 @@
     )(near, down)
 
 
+def to_column(row):
+    diagonal = iota((ROWS, ROWS), 0) == iota((ROWS, ROWS), 1)
+    return jnp.sum(jnp.where(diagonal, row, 0), axis=1, keepdims=True)
+
+
 def arrival_pick(pick, entry):
     return jnp.where(pick == entry, 1.0, 0.0).astype(BF)
 
 
-def attention_kernel(
-    pick_col, seg_row, seg_col, cos, sin, up, q, g, k, v, near, far, grad_out, lift_out,
-    gather, bias, lift, spread, spread_far
+STEP_HEADS = 2
+
+
+def head_grads(
+    step, i, up, q, g, k, v, near, far, grad_out, gather, bias, lift, spread, spread_far, cos, sin
 ):
-    step = pl.program_id(0)
-
-    @pl.when(step == 0)
-    def _():
-        gather[...] = arrival_pick(pick_col[...], iota((ROWS, ARRIVALS), 1))
-        allowed = (seg_col[...] == seg_row[...]) & (
-            iota((ROWS, ROWS), 0) <= iota((ROWS, ROWS), 1)
-        )
-        bias[...] = jnp.where(allowed, 0.0, -1e30)
-        lift[...] = jnp.zeros_like(lift)
-
-    columns = jnp.concatenate([q[...], g[...], k[...], v[...]], axis=1)
-    near_rows = gather_quarters(near[...], spread)
-    far_rows = gather_quarters(far[...], spread_far)
-    packed = dot(gather[...], jnp.concatenate([columns, near_rows, far_rows], axis=0)).astype(BF)
+    part, wide = columns(i, HEAD), columns(i, GROUP_WIDTH)
+    own_rows = jnp.concatenate([q[:, wide], g[:, wide], k[:, part], v[:, part]], axis=1)
+    near_rows = gather_quarters(near[:, :, columns(i, HEAD_QUARTER)], spread.at[i])
+    far_rows = gather_quarters(far[:, :, columns(i, HEAD_QUARTER)], spread_far.at[i])
+    packed = dot(gather[...], jnp.concatenate([own_rows, near_rows, far_rows], axis=0)).astype(BF)
     key = packed[:, 2 * GROUP_WIDTH : 2 * GROUP_WIDTH + HEAD]
     value = packed[:, 2 * GROUP_WIDTH + HEAD :]
     score_scale = 1.0 / math.sqrt(HEAD)
@@ -299,9 +305,11 @@
 
     key_grad = key_grad.astype(BF)
     value_grad = value_grad.astype(BF)
-    grad_out[:, pl.ds(pl.multiple_of(step * HEAD, HEAD), HEAD)] = key_grad
-    grad_out[:, pl.ds(pl.multiple_of(KEY_HEAD_WIDTH + step * HEAD, HEAD), HEAD)] = value_grad
-    up_rows = up[...]
+    grad_out[:, pl.ds(pl.multiple_of((step * STEP_HEADS + i) * HEAD, HEAD), HEAD)] = key_grad
+    grad_out[:, pl.ds(
+        pl.multiple_of(KEY_HEAD_WIDTH + (step * STEP_HEADS + i) * HEAD, HEAD), HEAD
+    )] = value_grad
+    up_rows = up[:, part]
     zero = jnp.zeros((ADAPTER_RANK, HEAD), BF)
     key_up = jnp.concatenate([up_rows[:ADAPTER_RANK], zero], axis=0)
     value_up = jnp.concatenate([zero, up_rows[ADAPTER_RANK:]], axis=0)
@@ -310,33 +318,51 @@
         jnp.concatenate([key_up, value_up], axis=1),
     )
 
-    @pl.when(step == KV_HEADS - 1)
+
+def attention_kernel(
+    pick_row, seg_row, cos, sin, up, q, g, k, v, near, far, grad_out, lift_out,
+    gather, bias, lift, spread, spread_far
+):
+    step = pl.program_id(0)
+
+    @pl.when(step == 0)
+    def _():
+        gather[...] = arrival_pick(to_column(pick_row[...]), iota((ROWS, ARRIVALS), 1))
+        allowed = (to_column(seg_row[...]) == seg_row[...]) & (
+            iota((ROWS, ROWS), 0) <= iota((ROWS, ROWS), 1)
+        )
+        bias[...] = jnp.where(allowed, 0.0, -1e30)
+        lift[...] = jnp.zeros_like(lift)
+
+    for i in range(STEP_HEADS):
+        head_grads(step, i, up, q, g, k, v, near, far, grad_out, gather, bias, lift, spread, spread_far, cos, sin)
+
+    @pl.when(step == KV_HEADS // STEP_HEADS - 1)
     def _():
         lift_out[...] = lift[...].astype(BF)
 
 
-def attention(pick_col, seg_row, seg_col, cos, sin, up, queries, grads, kv, near, far):
+def attention(pick_row, seg_row, cos, sin, up, queries, grads, kv, near, far):
     def whole(shape):
         return pl.BlockSpec(shape, lambda j: (0,) * len(shape))
 
     def head_block(width):
         return pl.BlockSpec((ROWS, width), lambda j: (0, j))
 
-    arrived = pl.BlockSpec((PEERS, 16, HEAD_QUARTER), lambda j: (0, 0, j))
+    arrived = pl.BlockSpec((PEERS, 16, STEP_HEADS * HEAD_QUARTER), lambda j: (0, 0, j))
     return pl.pallas_call(
         attention_kernel,
-        grid=(KV_HEADS,),
+        grid=(KV_HEADS // STEP_HEADS,),
         in_specs=[
-            whole((ROWS, 1)),
             whole((1, ROWS)),
-            whole((ROWS, 1)),
+            whole((1, ROWS)),
             whole((ROWS, HEAD)),
             whole((ROWS, HEAD)),
-            pl.BlockSpec((2 * ADAPTER_RANK, HEAD), lambda j: (0, j)),
-            head_block(GROUP_WIDTH),
-            head_block(GROUP_WIDTH),
-            head_block(HEAD),
-            pl.BlockSpec((ROWS, HEAD), lambda j: (0, KV_HEADS + j)),
+            pl.BlockSpec((2 * ADAPTER_RANK, STEP_HEADS * HEAD), lambda j: (0, j)),
+            head_block(STEP_HEADS * GROUP_WIDTH),
+            head_block(STEP_HEADS * GROUP_WIDTH),
+            head_block(STEP_HEADS * HEAD),
+            pl.BlockSpec((ROWS, STEP_HEADS * HEAD), lambda j: (0, KV_HEADS // STEP_HEADS + j)),
             arrived,
             arrived,
         ],
@@ -349,20 +375,20 @@
             pltpu.VMEM((ROWS, ARRIVALS), BF),
             pltpu.VMEM((ROWS, ROWS), F32),
             pltpu.VMEM((ROWS, HEAD), F32),
-            pltpu.VMEM((HEAD_QUARTER // HEAD, ROWS, HEAD), F32),
-            pltpu.VMEM((HEAD_QUARTER // HEAD, ROWS, HEAD), F32),
+            pltpu.VMEM((STEP_HEADS, HEAD_QUARTER // HEAD, ROWS, HEAD), F32),
+            pltpu.VMEM((STEP_HEADS, HEAD_QUARTER // HEAD, ROWS, HEAD), F32),
         ],
         compiler_params=pltpu.CompilerParams(vmem_limit_bytes=VMEM_LIMIT),
         cost_estimate=pl.CostEstimate(
             flops=12 * 10**9, bytes_accessed=14 * MIB, transcendentals=2 * 10**6
         ),
         name="attention_grads",
-    )(pick_col, seg_row, seg_col, cos, sin, up, queries, grads, kv, kv, near, far)
+    )(pick_row, seg_row, cos, sin, up, queries, grads, kv, kv, near, far)
 
 
 def adapter_kernel(
-    pick_row, pick_col, order_col, lift, own_down, near_down, near_x, far, x, kv_grad, out,
-    x_in, kv_in, far_in, near_in, placed_out, spread, load_sem, out_sem
+    pick_row, first_core, core_step, lift, own_down, near_down, near_x, far, x, kv_grad,
+    keep, give, x_in, kv_in, far_in, near_in, placed_out, spread, load_sem, out_sem
 ):
     loads = [
         pltpu.make_async_copy(far, far_in, load_sem.at[0]),
@@ -375,8 +401,21 @@
     for load in loads:
         load.start()
 
-    order = jnp.where(iota((BLOCK_ROWS, BLOCK_ROWS), 1) == order_col[...], 1.0, 0.0).astype(BF)
-    gather = arrival_pick(pick_col[...], iota((ROWS, ARRIVALS), 1))
+    core = lax.rem(lax.axis_index("local"), 2)
+    column = iota((PART_ROWS, PART_COLS), 1)
+    orders = [
+        jnp.concatenate(
+            [
+                jnp.where(
+                    column == first_core[...] + (at * core_step[...] + k * PART_SHIFT), 1.0, 0.0
+                ).astype(BF)
+                for at in (core, 1 - core)
+            ],
+            axis=0,
+        )
+        for k in range(PARTS)
+    ]
+    gather = arrival_pick(to_column(pick_row[...]), iota((ROWS, ARRIVALS), 1))
     spread_lift = arrival_pick(pick_row[...], iota((ARRIVALS, ROWS), 0))
     lifted = dot(spread_lift, lift[...]).astype(BF)
 
@@ -400,61 +439,61 @@
         loads[3 + z_lo].wait()
         arrived = jnp.concatenate([x_in[:, part], near_in[:, part], far_rows[:, part]], axis=0)
         down_sum = dot_tn(lifted, arrived).astype(BF)
-        both = jnp.concatenate(
-            [
-                jnp.concatenate(
-                    [
-                        down_sum[:, columns(y_high, DOWN_BLOCK)],
-                        up_sum[:, columns(2 * z_lo + y_high, UP_BLOCK)],
-                    ],
-                    axis=1,
+        rows = columns(z_lo, 2 * SHARD)
+        for k in range(PARTS):
+            y_low, x_high = k // 2, k % 2
+            both = []
+            for y_high in range(2):
+                start = y_high * DOWN_BLOCK + k * HEAD
+                both.append(
+                    jnp.concatenate(
+                        [
+                            down_sum[:, start : start + 2 * HEAD],
+                            up_sum[:, columns(2 * z_lo + y_high, UP_BLOCK)],
+                        ],
+                        axis=1,
+                    )
                 )
-                for y_high in range(2)
-            ],
-            axis=0,
-        )
-        placed = dot_nt(order, both).astype(BF)
-        rows = columns(z_lo, 2 * SHARD)
-        for y_high in range(2):
+            placed = dot_nt(orders[k], jnp.concatenate(both, axis=0)).astype(BF)
             for c in range(2):
-                for xx in range(4):
-                    for y_low in range(2):
-                        at = ((c * 4 + xx) * 2 + y_low) * 2 * SHARD
-                        placed_out[c, xx * 4 + y_high * 2 + y_low, rows, :] = placed[
+                for x_low in range(2):
+                    at = (c * 2 + x_low) * 2 * SHARD
+                    for y_high in range(2):
+                        y = y_high * 2 + y_low
+                        placed_out[c, (x_high * 2 + x_low) * 4 + y, rows, :] = placed[
                             at : at + 2 * SHARD, columns(y_high, HEAD)
                         ]
-        stores.append(
-            pltpu.make_async_copy(
-                placed_out.at[:, :, rows], out.at[:, :, rows], out_sem.at[z_lo]
+        for c, out in enumerate((give, keep)):
+            stores.append(
+                pltpu.make_async_copy(
+                    placed_out.at[1 - c, :, rows], out.at[:, rows], out_sem.at[2 * z_lo + c]
+                )
             )
-        )
-        stores[-1].start()
+            stores[-1].start()
     for store in stores:
         store.wait()
 
 
 def shard_order():
-    order = []
-    for c in range(2):
-        for xx in range(4):
-            for y_low in range(2):
-                for z_hi in range(2):
-                    device = ((y_low * 4 + xx) * 2 + z_hi) * 2 + c
-                    for r in range(DOWN_SHARD):
-                        order.append(device * DOWN_SHARD + r)
-                    for r in range(UP_SHARD):
-                        order.append(DOWN_BLOCK + device * UP_SHARD + r)
-    return np.asarray(order, np.int32).reshape(BLOCK_ROWS, 1)
-
-
-def adapters(pick_row, pick_col, lift, own_down, near_down, near_x, far, x, kv_grad):
+    order, step = [], []
+    for x_low in range(2):
+        for z_hi in range(2):
+            device = (x_low * 2 + z_hi) * 2
+            order += [device * DOWN_SHARD + r for r in range(DOWN_SHARD)]
+            order += [2 * HEAD + device * UP_SHARD + r for r in range(UP_SHARD)]
+            step += [DOWN_SHARD] * DOWN_SHARD + [UP_SHARD] * UP_SHARD
+    return [np.asarray(a, np.int32).reshape(PART_ROWS, 1) for a in (order, step)]
+
+
+def adapters(pick_row, lift, own_down, near_down, near_x, far, x, kv_grad):
     hbm, vmem = pl.BlockSpec(memory_space=pltpu.HBM), pl.BlockSpec(memory_space=pltpu.VMEM)
-    order_col = jnp.asarray(shard_order())
+    first_core, core_step = [jnp.asarray(a) for a in shard_order()]
+    half = jax.ShapeDtypeStruct((16, 8 * SHARD, HEAD), BF)
     return pl.pallas_call(
         adapter_kernel,
-        out_shape=jax.ShapeDtypeStruct((2, 16, 8 * SHARD, HEAD), BF),
+        out_shape=[half, half],
         in_specs=[vmem] * 6 + [hbm] * 4,
-        out_specs=hbm,
+        out_specs=[hbm, hbm],
         scratch_shapes=[
             pltpu.VMEM((ROWS, MODEL_WIDTH), BF),
             pltpu.VMEM((ROWS, 2 * KEY_HEAD_WIDTH), BF),
@@ -463,14 +502,25 @@
             pltpu.VMEM((2, 16, 8 * SHARD, HEAD), BF),
             pltpu.VMEM((X_QUARTER // HEAD, ROWS, HEAD), F32),
             pltpu.SemaphoreType.DMA((3 + QUARTERS,)),
-            pltpu.SemaphoreType.DMA((BLOCK_COUNT // 2,)),
+            pltpu.SemaphoreType.DMA((BLOCK_COUNT,)),
         ],
         compiler_params=pltpu.CompilerParams(vmem_limit_bytes=VMEM_LIMIT),
         cost_estimate=pl.CostEstimate(
             flops=4 * 10**9, bytes_accessed=10 * MIB, transcendentals=0
         ),
         name="adapter_grads",
-    )(pick_row, pick_col, order_col, lift, own_down, near_down, near_x, far, x, kv_grad)
+    )(
+        pick_row,
+        first_core,
+        core_step,
+        lift,
+        own_down,
+        near_down,
+        near_x,
+        far,
+        x,
+        kv_grad,
+    )
 
 
 def device_groups(axes):
@@ -493,9 +543,9 @@
     )
 
 
-def sum_over_devices(parts):
-    both = exchange(parts, ["core"])
-    total = (both[0].astype(F32) + both[1].astype(F32)).astype(BF)
+def sum_over_devices(keep, give):
+    got = lax.ppermute(give, ("node", "local"), [(i, i ^ 1) for i in range(256)])
+    total = (keep.astype(F32) + got.astype(F32)).astype(BF)
     total = jnp.sum(exchange(total, ["x", "y"]).astype(F32), axis=0)
     total = total.reshape(8, SHARD, HEAD)
     return jnp.sum(exchange(total, ["z_lo", "z_hi"]), axis=0)
@@ -528,35 +578,26 @@
     arrival_pick_index,
     packed_sequence_number,
 ):
-    own_local = lax.axis_index("local")
-    own_node = lax.axis_index("node")
-    moved_in = bin_local_index != own_local
-    moved_out = jnp.logical_not(moved_in) & (spill_node != own_node)
-    near_target = jnp.where(moved_in, bin_local_index * CAP_L + bin_row_offset, -1)
-    far_target = jnp.where(moved_out, spill_node * CAP_N + spill_row_offset, -1)
-
+    plan = (bin_local_index, bin_row_offset, spill_node, spill_row_offset)
     rows = (queries, attention_out_grad, rotated_key_value, activations)
-    (near_send,) = pack(near_target, *rows)
-    far_send, far_x_send, own_down = pack(far_target, *rows, adapter_down)
+    (near_send,) = pack(plan, *rows)
+    far_send, far_x_send, own_down = pack(plan, *rows, adapter_down)
 
     near = lax.all_to_all(near_send, "local", split_axis=0, concat_axis=0, tiled=True)
     far_send, near = lax.optimization_barrier((far_send, near))
     far = lax.all_to_all(far_send, "node", split_axis=0, concat_axis=0, tiled=True)
     near_x, near_down = near_adapter_rows(near[:, :, ATT_COLS:], adapter_down)
     pick_row = arrival_pick_index
-    pick_col = arrival_pick_index.reshape(ROWS, 1)
     seg_row = packed_sequence_number
-    seg_col = packed_sequence_number.reshape(ROWS, 1)
     cos, sin = rope_tables(packed_sequence_number.reshape(-1))
-    far_x_send, far, near_x, near_down, pick_col, seg_col, cos, sin = lax.optimization_barrier(
-        (far_x_send, far, near_x, near_down, pick_col, seg_col, cos, sin)
+    far_x_send, far, near_x, near_down, cos, sin = lax.optimization_barrier(
+        (far_x_send, far, near_x, near_down, cos, sin)
     )
     far_x = lax.all_to_all(far_x_send, "node", split_axis=0, concat_axis=0, tiled=True)
 
     kv_grad, lift = attention(
-        pick_col,
+        pick_row,
         seg_row,
-        seg_col,
         cos,
         sin,
         adapter_up,
@@ -566,9 +607,8 @@
         near,
         far,
     )
-    parts = adapters(
+    keep, give = adapters(
         pick_row,
-        pick_col,
         lift,
         own_down,
         near_down,
@@ -577,7 +617,7 @@
         activations,
         kv_grad,
     )
-    total = sum_over_devices(parts) * (1.0 / math.sqrt(256 * ROWS))
+    total = sum_over_devices(keep, give) * (1.0 / math.sqrt(256 * ROWS))
     return (kv_grad, total[:DOWN_SHARD], total[DOWN_SHARD:])
 
 

time: 189 us -> 182 us (0.963)
  blocking collectives: 38.1 us -> 30.2 us
  waiting for transfers between devices: 54.6 us -> 58.8 us
  Pallas kernels: 42 us -> 39.9 us
    all_to_all x3 -> x2, blocking collectives: 38.1 us -> 30.2 us  [exchange(): lax.all_to_all(array, ('node', 'local'), split_axis=0, concat_axis=0, axi...]
    ppermute x0 -> x1, waiting for transfers between devices: none -> 2.48 us  [sum_over_devices(): lax.ppermute(give, ('node', 'local'), [(i, i ^ 1) for i in range(256)])]
    pallas_call x4, Pallas kernels: 39.3 us -> 37.2 us  [the longest x1 16.2 us: attention(): pl.pallas_call(attention_kernel, grid=(KV_HEADS // STEP_HEADS,), in_specs...]
  transfers between devices with their start and end apart: 3 -> 4, of which waited for: 2 -> 4; matrix products, arithmetic and copies ran while one was open for 3% -> 2% of each run, Pallas kernels for 15% -> 15%
where the time goes in v2:
time: 182 us; the launch traced here: 180 us
  waiting for transfers between devices  58.8 us (32%)
  starting transfers between devices  45.1 us (25%)
  Pallas kernels  39.9 us (22%)
  blocking collectives  30.2 us (17%)
  other arithmetic  3.03 us (2%)
  local copies, waits for them, and re-layouts  2.57 us (1%)
    all_to_all x2, blocking collectives, exchange(): lax.all_to_all(array, ('node', 'local'), split_axis=0, concat_axis=0, axi...  30.2 us
    all_to_all x1, waiting for transfers between devices, local(): lax.all_to_all(near_send, 'local', split_axis=0, concat_axis=0, tiled=True)  27.3 us
    all_to_all x1, waiting for transfers between devices, local(): lax.all_to_all(far_send, 'node', split_axis=0, concat_axis=0, tiled=True)  27.3 us
    all_to_all x1, starting transfers between devices, local(): lax.all_to_all(far_send, 'node', split_axis=0, concat_axis=0, tiled=True)  25.2 us
    pallas_call x1, Pallas kernels, attention(): pl.pallas_call(attention_kernel, grid=(KV_HEADS // STEP_HEADS,), in_specs...  16.2 us
    pallas_call x2, Pallas kernels, pack(): pl.pallas_call(functools.partial(pack_kernel, near), in_specs=[vmem] * 4...  14.5 us
    all_to_all x1, starting transfers between devices, local(): lax.all_to_all(near_send, 'local', split_axis=0, concat_axis=0, tiled=True)  11.5 us
    all_to_all x1, starting transfers between devices, local(): lax.all_to_all(far_x_send, 'node', split_axis=0, concat_axis=0, tiled=True)  8.3 us
  transfers between devices with their start and end apart: 4, of which 4 were waited for; matrix products, arithmetic and copies ran while one was open for 2% of the time, Pallas kernels for 15%

profile of v2, /device:TPU:2, one launch (start us, length us, event | category | flops | bytes accessed | tf_op | source)
XLA Modules:
  0.0 180.4 jit_solution(2278934413302955931)
XLA Ops:
  0.6 6.3 %pack_rows.3 = bf16[16,16,4352]{2,1,0:T(8,128)(2,1)} custom-call(s32[1,256]{1,0:T(1,128)} %bin_local.3, s32[1,256]{1,0:T(1,128)} %bin_offset.3, s32[1,256]{1,0:T(1,128)} %spill_node.3, s32[1,256]{1,0:T(1,128)} %spill_offset.3, bf16[256,5120]{1,0:T(8,128)(2,1)} %q.5, bf16[256,5120]{1,0:T(8,128)(2,1)} %g.5, bf16[256,2048]{1,0:T(8,128)(2,1)} %v.1, ...), custom_call_target="tpu_custom_call" | custom-call | flops 570425344 | bytes 14680064 | tf_op jit(solution)/shard_map/pack_rows/pallas_call | solution.py:209
  6.9 11.5 %all-to-all-start = ((bf16[16,16,4352]{2,1,0:T(8,128)(2,1)}), bf16[16,16,4352]{2,1,0:T(8,128)(2,1)}, u32[]{:S(2)}, u32[]{:S(2)}) async-start(bf16[16,16,4352]{2,1,0:T(8,128)(2,1)} %pack_rows.3), calls=%async_computation | async-start | bytes 4456448 | tf_op jit(solution)/shard_map/all_to_all | solution.py:586
  18.4 8.2 %pack_rows.2 = (bf16[16,16,3072]{2,1,0:T(8,128)(2,1)}, bf16[16,16,1408]{2,1,0:T(8,128)(2,1)}, bf16[256,128]{1,0:T(8,128)(2,1)}) custom-call(s32[1,256]{1,0:T(1,128)} %bin_local.3, s32[1,256]{1,0:T(1,128)} %bin_offset.3, s32[1,256]{1,0:T(1,128)} %spill_node.3, s32[1,256]{1,0:T(1,128)} %spill_offset.3, bf16[256,5120]{1,0:T(8,128)(2,1)} %q.5, ...), custom_call_target="tpu_custom_call" | custom-call | flops 570425344 | bytes 14680064 | tf_op jit(solution)/shard_map/pack_rows/pallas_call | solution.py:209
  26.6 27.3 %all-to-all-done.near = bf16[16,16,4352]{2,1,0:T(8,128)(2,1)} async-done(((bf16[16,16,4352]{2,1,0:T(8,128)(2,1)}), bf16[16,16,4352]{2,1,0:T(8,128)(2,1)}, u32[]{:S(2)}, u32[]{:S(2)}) %all-to-all-start) | async-done | bytes 2228256 | tf_op jit(solution)/shard_map/all_to_all | solution.py:586
  53.9 0.0 copy-start.2
  53.9 25.2 %all-to-all-start.1 = ((bf16[16,16,3072]{2,1,0:T(8,128)(2,1)}), bf16[16,16,3072]{2,1,0:T(8,128)(2,1)S(1)}, u32[]{:S(2)}, u32[]{:S(2)}) async-start(bf16[16,16,3072]{2,1,0:T(8,128)(2,1)} %get-tuple-element.22), calls=%async_computation.1 | async-start | bytes 3145728 | tf_op jit(solution)/shard_map/all_to_all | solution.py:588
  79.2 0.0 copy-done.2
  79.2 0.2 convert_reduce_fusion.1
  79.4 0.5 multiply_sine_fusion
  79.9 0.8 pad_maximum_fusion
  80.7 2.0 %slice.9.near = bf16[16,16,1280]{2,1,0:T(8,128)(2,1)} slice(bf16[16,16,4352]{2,1,0:T(8,128)(2,1)} %all-to-all-done.near), slice={[0:16], [0:16], [3072:4352]} | slice | bytes 1310720 | tf_op jit(solution)/shard_map/slice | solution.py:589
  82.7 2.7 %near_adapter_rows.1 = (bf16[64,5120]{1,0:T(8,128)(2,1)}, bf16[64,128]{1,0:T(8,128)(2,1)}) custom-call(bf16[16,16,1280]{2,1,0:T(8,128)(2,1)} %slice.9.near, bf16[5120,128]{1,0:T(8,128)(2,1)} %down.1), custom_call_target="tpu_custom_call" | custom-call | flops 83886080 | bytes 3145728 | tf_op jit(solution)/shard_map/near_adapter_rows/pallas_call | solution.py:232
  85.4 27.3 %all-to-all-done.1.far = bf16[16,16,3072]{2,1,0:T(8,128)(2,1)S(1)} async-done(((bf16[16,16,3072]{2,1,0:T(8,128)(2,1)}), bf16[16,16,3072]{2,1,0:T(8,128)(2,1)S(1)}, u32[]{:S(2)}, u32[]{:S(2)}) %all-to-all-start.1) | async-done | bytes 1572896 | tf_op jit(solution)/shard_map/all_to_all | solution.py:588
  112.6 0.0 copy-start
  112.6 8.3 %all-to-all-start.2 = ((bf16[16,16,1408]{2,1,0:T(8,128)(2,1)}), bf16[16,16,1408]{2,1,0:T(8,128)(2,1)}, u32[]{:S(2)}, u32[]{:S(2)}) async-start(bf16[16,16,1408]{2,1,0:T(8,128)(2,1)} %get-tuple-element.34), calls=%async_computation.2 | async-start | bytes 1441792 | tf_op jit(solution)/shard_map/all_to_all | solution.py:596
  120.9 0.0 copy-done
  121.0 16.2 %attention_grads.1 = (bf16[256,2048]{1,0:T(8,128)(2,1)}, bf16[256,128]{1,0:T(8,128)(2,1)}) custom-call(s32[1,256]{1,0:T(1,128)} %pick_row.3, s32[1,256]{1,0:T(1,128)} %seg_row.1, f32[256,128]{1,0:T(8,128)} %get-tuple-element.26.cos, f32[256,128]{1,0:T(8,128)} %get-tuple-element.27.sin, bf16[128,1024]{1,0:T(8,128)(2,1)} %up.1, bf16[256,5120]{1,0:T(8,128)(2,1)} %q.5, ...), custom_call_target="tpu_custom_call" | custom-call | flops 12000000000 | bytes 14680064 | tf_op jit(solution)/shard_map/attention_grads/pallas_call | solution.py:353
  137.2 1.8 %all-to-all-done.2.far = bf16[16,16,1408]{2,1,0:T(8,128)(2,1)} async-done(((bf16[16,16,1408]{2,1,0:T(8,128)(2,1)}), bf16[16,16,1408]{2,1,0:T(8,128)(2,1)}, u32[]{:S(2)}, u32[]{:S(2)}) %all-to-all-start.2) | async-done | bytes 720928 | tf_op jit(solution)/shard_map/all_to_all | solution.py:596
  139.0 6.5 %adapter_grads.1 = (bf16[16,192,128]{2,1,0:T(8,128)(2,1)}, bf16[16,192,128]{2,1,0:T(8,128)(2,1)}) custom-call(s32[1,256]{1,0:T(1,128)} %pick_row.3, s32[96,1]{1,0:T(8,128)} %constant.17.clone.first_core, s32[96,1]{1,0:T(8,128)} %constant.18.clone.core_step, bf16[256,128]{1,0:T(8,128)(2,1)} %get-tuple-element.30.lift, ...), custom_call_target="tpu_custom_call" | custom-call | flops 4000000000 | bytes 10485760 | tf_op jit(solution)/shard_map/adapter_grads/pallas_call | solution.py:492
  145.5 0.1 collective-permute-start
  145.6 2.5 %collective-permute-done = bf16[16,192,128]{2,1,0:T(8,128)(2,1)S(1)} collective-permute-done((bf16[16,192,128]{2,1,0:T(8,128)(2,1)}, bf16[16,192,128]{2,1,0:T(8,128)(2,1)S(1)}, u32[]{:S(2)}, u32[]{:S(2)}) %collective-permute-start) | collective-permute-done | bytes 786464 | tf_op jit(solution)/shard_map/ppermute | solution.py:547
  148.1 1.3 add_convert_fusion
  149.4 18.8 %all_to_all.25 = bf16[16,192,128]{2,1,0:T(8,128)(2,1)S(1)} all-to-all(bf16[16,192,128]{2,1,0:T(8,128)(2,1)S(1)} %add_convert_fusion), channel_id=1, replica_groups={{0,16,32,48,4,20,36,52,8,24,40,56,12,28,44,60},{1,17,33,49,5,21,37,53,9..., dimensions={0} | all-to-all | bytes 1572864 | tf_op jit(solution)/shard_map/all_to_all | solution.py:536
  168.2 0.1 convert_reduce_fusion
  168.3 11.4 %all_to_all.26 = f32[8,24,128]{2,1,0:T(8,128)S(1)} all-to-all(f32[8,24,128]{2,1,0:T(8,128)S(1)} %bitcast.3), channel_id=1, replica_groups={{0,2,64,66,128,130,192,194},{1,3,65,67,129,131,193,195},{4,6,68,70,132,..., dimensions={0} | all-to-all | bytes 196608 | tf_op jit(solution)/shard_map/all_to_all | solution.py:536
  179.7 0.0 copy-start.1
  179.8 0.6 slice.13
  180.3 0.0 copy-done.1
  (4 shorter events, 0.0 us)
Async XLA Ops:
  6.9 47.0 %all-to-all-start = ((bf16[16,16,4352]{2,1,0:T(8,128)(2,1)}), bf16[16,16,4352]{2,1,0:T(8,128)(2,1)}, u32[]{:S(2)}, u32[]{:S(2)}) async-start(bf16[16,16,4352]{2,1,0:T(8,128)(2,1)} %pack_rows.3), calls=%async_computation | async-start | bytes 4456448 | tf_op jit(solution)/shard_map/all_to_all | solution.py:586
  53.9 25.2 %copy-start.2 = (s32[1,256]{1,0:T(1,128)S(1)}, s32[1,256]{1,0:T(1,128)}, u32[]{:S(2)}) copy-start(s32[1,256]{1,0:T(1,128)} %seg_row.1) | copy-start | bytes 3076
  53.9 58.7 %all-to-all-start.1 = ((bf16[16,16,3072]{2,1,0:T(8,128)(2,1)}), bf16[16,16,3072]{2,1,0:T(8,128)(2,1)S(1)}, u32[]{:S(2)}, u32[]{:S(2)}) async-start(bf16[16,16,3072]{2,1,0:T(8,128)(2,1)} %get-tuple-element.22), calls=%async_computation.1 | async-start | bytes 3145728 | tf_op jit(solution)/shard_map/all_to_all | solution.py:588
  112.6 8.3 %copy-start = (bf16[16,16,3072]{2,1,0:T(8,128)(2,1)}, bf16[16,16,3072]{2,1,0:T(8,128)(2,1)S(1)}, u32[]{:S(2)}) copy-start(bf16[16,16,3072]{2,1,0:T(8,128)(2,1)S(1)} %all-to-all-done.1.far) | copy-start | bytes 4718596
  112.6 26.4 %all-to-all-start.2 = ((bf16[16,16,1408]{2,1,0:T(8,128)(2,1)}), bf16[16,16,1408]{2,1,0:T(8,128)(2,1)}, u32[]{:S(2)}, u32[]{:S(2)}) async-start(bf16[16,16,1408]{2,1,0:T(8,128)(2,1)} %get-tuple-element.34), calls=%async_computation.2 | async-start | bytes 1441792 | tf_op jit(solution)/shard_map/all_to_all | solution.py:596
  145.5 2.6 %collective-permute-start = (bf16[16,192,128]{2,1,0:T(8,128)(2,1)}, bf16[16,192,128]{2,1,0:T(8,128)(2,1)S(1)}, u32[]{:S(2)}, u32[]{:S(2)}) collective-permute-start(bf16[16,192,128]{2,1,0:T(8,128)(2,1)} %get-tuple-element.36), channel_id=1, source_target_pairs={{0,1},{1,0},{2,3},{3,2},{4,5},{5,4},{6,7},{7,6},{8,9},{9,8},{10,11... | collective-permute-start | bytes 2359304 | tf_op jit(solution)/shard_map/ppermute | solution.py:547
  179.7 0.6 copy-start.1

commit v3 on v2

--- a/solution.py
+++ b/solution.py
@@ -103,7 +103,7 @@
         att_out, *rest = rest
         x_out, x_from = att_out, ATT_COLS
     else:
-        down, att_out, x_out, down_out, *rest = rest
+        down, att_out, x_out, *rest = rest
         x_from = 0
     q_in, g_in, kv_in, x_in, att, att_x, spread, spread_x, head_sem, x_sem, out_sem, *rest = rest
 
@@ -156,18 +156,23 @@
         send(att.at[:, :, part], att_out.at[:, :, part], out_sem.at[j])
     for load in x_loads:
         load.wait()
+    moved_down = 0.0
     for j in range(X_STEPS):
         rows = jnp.concatenate(
             [x_in[:, columns(c * X_STEPS + j, X_STEP)] for c in range(QUARTERS)], axis=1
         )
         part = columns(j, X_STEP)
-        att_x[:, :, part] = interleave(dot(select, rows), spread_x.at[j % 2])
+        picked = dot(select, rows)
+        att_x[:, :, part] = interleave(picked, spread_x.at[j % 2])
+        if not near:
+            down_rows = jnp.concatenate(
+                [down_in[columns(c * X_STEPS + j, X_STEP)] for c in range(QUARTERS)], axis=0
+            )
+            moved_down = moved_down + dot(picked.astype(BF), down_rows)
         to = slice(x_from + part.start, x_from + part.stop)
         send(att_x.at[:, :, part], x_out.at[:, :, to], out_sem.at[KV_HEADS + j])
     if not near:
-        own_out = dot(x_in[...], down_in[...]).astype(BF)
-        down_out[...] = own_out
-        picked = dot(select, own_out)
+        picked = moved_down.astype(BF).astype(F32)
         rows = jnp.concatenate([picked] + [jnp.zeros_like(picked)] * (QUARTERS - 1), axis=1)
         att_down[...] = interleave(rows, spread_x.at[0, :1])
         send(att_down, x_out.at[:, :, X_QUARTER:], down_sem.at[1])
@@ -195,11 +200,10 @@
         args, out_specs = (), [hbm]
         out_shape = [jax.ShapeDtypeStruct((PEERS, 16, ATT_COLS + X_QUARTER), BF)]
     else:
-        args, out_specs = (down,), [hbm, hbm, vmem]
+        args, out_specs = (down,), [hbm, hbm]
         out_shape = [
             jax.ShapeDtypeStruct((PEERS, 16, ATT_COLS), BF),
             jax.ShapeDtypeStruct((PEERS, 16, X_QUARTER + HEAD), BF),
-            jax.ShapeDtypeStruct((ROWS, HEAD), BF),
         ]
         scratch += [
             pltpu.VMEM((MODEL_WIDTH, HEAD), BF),
@@ -222,35 +226,37 @@
     )(*plan, queries, grads, kv, activations, *args)
 
 
-def near_kernel(near, down, x_out, down_out, spread):
+def near_kernel(near, x, down, near_x_out, down_out, spread):
     rows = gather_quarters(near[...], spread)
-    x_out[...] = rows
-    down_out[...] = dot(rows, down[...]).astype(BF)
-
-
-def near_adapter_rows(near, down):
+    near_x_out[...] = rows
+    down_out[:ROWS] = dot(x[...], down[...]).astype(BF)
+    down_out[ROWS:] = dot(rows, down[...]).astype(BF)
+
+
+def near_adapter_rows(near, x, down):
+    def whole(*shape):
+        return pl.BlockSpec(shape, lambda i: (0,) * len(shape))
+
     return pl.pallas_call(
         near_kernel,
         grid=(1,),
         in_specs=[
-            pl.BlockSpec((PEERS, 16, X_QUARTER), lambda i: (0, 0, 0)),
-            pl.BlockSpec((MODEL_WIDTH, HEAD), lambda i: (0, 0)),
+            whole(PEERS, 16, X_QUARTER),
+            whole(ROWS, MODEL_WIDTH),
+            whole(MODEL_WIDTH, HEAD),
         ],
-        out_specs=[
-            pl.BlockSpec((MOVED, MODEL_WIDTH), lambda i: (0, 0)),
-            pl.BlockSpec((MOVED, HEAD), lambda i: (0, 0)),
-        ],
+        out_specs=[whole(MOVED, MODEL_WIDTH), whole(ROWS + MOVED, HEAD)],
         out_shape=[
-            jax.ShapeDtypeStruct((MOVED, MODEL_WIDTH), BF),
-            jax.ShapeDtypeStruct((MOVED, HEAD), BF),
+            jax.ShapeDtypeStruct((MOVED, 40 * MODEL_WIDTH), BF),
+            jax.ShapeDtypeStruct((ROWS + MOVED, HEAD), BF),
         ],
         scratch_shapes=[pltpu.VMEM((X_QUARTER // HEAD, ROWS, HEAD), F32)],
-        compiler_params=pltpu.CompilerParams(vmem_limit_bytes=VMEM_LIMIT),
+        compiler_params=pltpu.CompilerParams(vmem_limit_bytes=32 * MIB),
         cost_estimate=pl.CostEstimate(
-            flops=2 * MOVED * MODEL_WIDTH * HEAD, bytes_accessed=3 * MIB, transcendentals=0
+            flops=2 * MOVED * MODEL_WIDTH * HEAD, bytes_accessed=9 * MIB, transcendentals=0
         ),
         name="near_adapter_rows",
-    )(near, down)
+    )(near, x, down)
 
 
 def to_column(row):
@@ -369,7 +375,7 @@
         out_specs=[whole((ROWS, 2 * KEY_HEAD_WIDTH)), whole((ROWS, HEAD))],
         out_shape=[
             jax.ShapeDtypeStruct((ROWS, 2 * KEY_HEAD_WIDTH), BF),
-            jax.ShapeDtypeStruct((ROWS, HEAD), BF),
+            jax.ShapeDtypeStruct((ROWS, 384 * HEAD), BF),
         ],
         scratch_shapes=[
             pltpu.VMEM((ROWS, ARRIVALS), BF),
@@ -378,7 +384,7 @@
             pltpu.VMEM((STEP_HEADS, HEAD_QUARTER // HEAD, ROWS, HEAD), F32),
             pltpu.VMEM((STEP_HEADS, HEAD_QUARTER // HEAD, ROWS, HEAD), F32),
         ],
-        compiler_params=pltpu.CompilerParams(vmem_limit_bytes=VMEM_LIMIT),
+        compiler_params=pltpu.CompilerParams(vmem_limit_bytes=54 * MIB),
         cost_estimate=pl.CostEstimate(
             flops=12 * 10**9, bytes_accessed=14 * MIB, transcendentals=2 * 10**6
         ),
@@ -387,17 +393,20 @@
 
 
 def adapter_kernel(
-    pick_row, first_core, core_step, lift, own_down, near_down, near_x, far, x, kv_grad,
-    keep, give, x_in, kv_in, far_in, near_in, placed_out, spread, load_sem, out_sem
+    pick_row, first_core, core_step, near_down, x, far, lift, near_x, kv_grad,
+    keep, give, _kv_grad, lift_in, near_in, kv_in, far_in, placed_out, spread, load_sem, out_sem
 ):
     loads = [
-        pltpu.make_async_copy(far, far_in, load_sem.at[0]),
-        pltpu.make_async_copy(kv_grad, kv_in, load_sem.at[1]),
-        pltpu.make_async_copy(near_x, near_in, load_sem.at[2]),
+        pltpu.make_async_copy(source, to, load_sem.at[i])
+        for i, (source, to) in enumerate(
+            (
+                (lift.at[:, :HEAD], lift_in),
+                (far, far_in),
+                (kv_grad, kv_in),
+                (near_x.at[:, :MODEL_WIDTH], near_in),
+            )
+        )
     ]
-    for c in range(QUARTERS):
-        part = columns(c, X_QUARTER)
-        loads.append(pltpu.make_async_copy(x.at[:, part], x_in.at[:, part], load_sem.at[3 + c]))
     for load in loads:
         load.start()
 
@@ -417,27 +426,27 @@
     ]
     gather = arrival_pick(to_column(pick_row[...]), iota((ROWS, ARRIVALS), 1))
     spread_lift = arrival_pick(pick_row[...], iota((ARRIVALS, ROWS), 0))
-    lifted = dot(spread_lift, lift[...]).astype(BF)
-
     loads[0].wait()
+    lifted = dot(spread_lift, lift_in[...]).astype(BF)
+
+    loads[1].wait()
     far_rows = gather_quarters(far_in[:, :, :X_QUARTER], spread)
     spread[0] = far_in[:, :, X_QUARTER:].reshape(ROWS, HEAD).astype(F32)
     far_down = spread[0, pl.ds(0, MOVED, stride=QUARTERS), :].astype(BF)
 
-    arrived_down = jnp.concatenate([own_down[...], near_down[...], far_down], axis=0)
+    arrived_down = jnp.concatenate([near_down[...], far_down], axis=0)
     down_out = dot(gather, arrived_down).astype(BF)
-    loads[1].wait()
+    loads[2].wait()
     up_both = dot_tn(down_out, kv_in[...])
     up_sum = jnp.concatenate(
         [up_both[:ADAPTER_RANK, :KEY_HEAD_WIDTH], up_both[ADAPTER_RANK:, KEY_HEAD_WIDTH:]], axis=0
     ).astype(BF)
 
-    loads[2].wait()
+    loads[3].wait()
     stores = []
     for z_lo in range(BLOCK_COUNT // 2):
         part = columns(z_lo, X_QUARTER)
-        loads[3 + z_lo].wait()
-        arrived = jnp.concatenate([x_in[:, part], near_in[:, part], far_rows[:, part]], axis=0)
+        arrived = jnp.concatenate([x[:, part], near_in[:, part], far_rows[:, part]], axis=0)
         down_sum = dot_tn(lifted, arrived).astype(BF)
         rows = columns(z_lo, 2 * SHARD)
         for k in range(PARTS):
@@ -485,42 +494,34 @@
     return [np.asarray(a, np.int32).reshape(PART_ROWS, 1) for a in (order, step)]
 
 
-def adapters(pick_row, lift, own_down, near_down, near_x, far, x, kv_grad):
+def adapters(pick_row, near_down, x, far, lift, near_x, kv_grad):
     hbm, vmem = pl.BlockSpec(memory_space=pltpu.HBM), pl.BlockSpec(memory_space=pltpu.VMEM)
+    place = pl.BlockSpec(memory_space=pl.ANY)
     first_core, core_step = [jnp.asarray(a) for a in shard_order()]
     half = jax.ShapeDtypeStruct((16, 8 * SHARD, HEAD), BF)
+    passed = jax.ShapeDtypeStruct(kv_grad.shape, kv_grad.dtype)
     return pl.pallas_call(
         adapter_kernel,
-        out_shape=[half, half],
-        in_specs=[vmem] * 6 + [hbm] * 4,
-        out_specs=[hbm, hbm],
+        out_shape=[half, half, passed],
+        input_output_aliases={8: 2},
+        in_specs=[vmem] * 5 + [hbm] * 4,
+        out_specs=[place, place, hbm],
         scratch_shapes=[
-            pltpu.VMEM((ROWS, MODEL_WIDTH), BF),
+            pltpu.VMEM((ROWS, HEAD), BF),
+            pltpu.VMEM((MOVED, MODEL_WIDTH), BF),
             pltpu.VMEM((ROWS, 2 * KEY_HEAD_WIDTH), BF),
             pltpu.VMEM((PEERS, 16, X_QUARTER + HEAD), BF),
-            pltpu.VMEM((MOVED, MODEL_WIDTH), BF),
             pltpu.VMEM((2, 16, 8 * SHARD, HEAD), BF),
             pltpu.VMEM((X_QUARTER // HEAD, ROWS, HEAD), F32),
-            pltpu.SemaphoreType.DMA((3 + QUARTERS,)),
+            pltpu.SemaphoreType.DMA((4,)),
             pltpu.SemaphoreType.DMA((BLOCK_COUNT,)),
         ],
-        compiler_params=pltpu.CompilerParams(vmem_limit_bytes=VMEM_LIMIT),
+        compiler_params=pltpu.CompilerParams(vmem_limit_bytes=40 * MIB),
         cost_estimate=pl.CostEstimate(
             flops=4 * 10**9, bytes_accessed=10 * MIB, transcendentals=0
         ),
         name="adapter_grads",
-    )(
-        pick_row,
-        first_core,
-        core_step,
-        lift,
-        own_down,
-        near_down,
-        near_x,
-        far,
-        x,
-        kv_grad,
-    )
+    )(pick_row, first_core, core_step, near_down, x, far, lift, near_x, kv_grad)
 
 
 def device_groups(axes):
@@ -581,12 +582,12 @@
     plan = (bin_local_index, bin_row_offset, spill_node, spill_row_offset)
     rows = (queries, attention_out_grad, rotated_key_value, activations)
     (near_send,) = pack(plan, *rows)
-    far_send, far_x_send, own_down = pack(plan, *rows, adapter_down)
+    far_send, far_x_send = pack(plan, *rows, adapter_down)
 
     near = lax.all_to_all(near_send, "local", split_axis=0, concat_axis=0, tiled=True)
     far_send, near = lax.optimization_barrier((far_send, near))
     far = lax.all_to_all(far_send, "node", split_axis=0, concat_axis=0, tiled=True)
-    near_x, near_down = near_adapter_rows(near[:, :, ATT_COLS:], adapter_down)
+    near_x, near_down = near_adapter_rows(near[:, :, ATT_COLS:], activations, adapter_down)
     pick_row = arrival_pick_index
     seg_row = packed_sequence_number
     cos, sin = rope_tables(packed_sequence_number.reshape(-1))
@@ -607,15 +608,8 @@
         near,
         far,
     )
-    keep, give = adapters(
-        pick_row,
-        lift,
-        own_down,
-        near_down,
-        near_x,
-        far_x,
-        activations,
-        kv_grad,
+    keep, give, kv_grad = adapters(
+        pick_row, near_down, activations, far_x, lift, near_x, kv_grad
     )
     total = sum_over_devices(keep, give) * (1.0 / math.sqrt(256 * ROWS))
     return (kv_grad, total[:DOWN_SHARD], total[DOWN_SHARD:])

time: 182 us -> 179 us (0.984)
  Pallas kernels: 39.9 us -> 37.1 us
  waiting for transfers between devices: 58.8 us -> 60.9 us
    pallas_call x2, Pallas kernels: 9.18 us -> 7.09 us  [the longest x1 5.2 us: adapters(): pl.pallas_call(adapter_kernel, out_shape=[half, half, passed], input_outp...]
  transfers between devices with their start and end apart: 4 -> 4, of which waited for: 4 -> 4; matrix products, arithmetic and copies ran while one was open for 2% -> 2% of each run, Pallas kernels for 15% -> 14%
where the time goes in v3:
time: 179 us; the launch traced here: 178 us
  waiting for transfers between devices  60.9 us (34%)
  starting transfers between devices  45.2 us (25%)
  Pallas kernels  37.1 us (21%)
  blocking collectives  30.6 us (17%)
  other arithmetic  1.9 us (1%)
    all_to_all x2, blocking collectives, exchange(): lax.all_to_all(array, ('node', 'local'), split_axis=0, concat_axis=0, axi...  30.6 us
    all_to_all x1, waiting for transfers between devices, local(): lax.all_to_all(far_send, 'node', split_axis=0, concat_axis=0, tiled=True)  28.9 us
    all_to_all x1, waiting for transfers between devices, local(): lax.all_to_all(near_send, 'local', split_axis=0, concat_axis=0, tiled=True)  28.2 us
    all_to_all x1, starting transfers between devices, local(): lax.all_to_all(far_send, 'node', split_axis=0, concat_axis=0, tiled=True)  25.4 us
    pallas_call x1, Pallas kernels, attention(): pl.pallas_call(attention_kernel, grid=(KV_HEADS // STEP_HEADS,), in_specs...  16.5 us
    pallas_call x2, Pallas kernels, pack(): pl.pallas_call(functools.partial(pack_kernel, near), in_specs=[vmem] * 4...  13.5 us
    all_to_all x1, starting transfers between devices, local(): lax.all_to_all(near_send, 'local', split_axis=0, concat_axis=0, tiled=True)  11.5 us
    all_to_all x1, starting transfers between devices, local(): lax.all_to_all(far_x_send, 'node', split_axis=0, concat_axis=0, tiled=True)  8.25 us
  transfers between devices with their start and end apart: 4, of which 4 were waited for; matrix products, arithmetic and copies ran while one was open for 2% of the time, Pallas kernels for 14%

profile of v3, /device:TPU:2, one launch (start us, length us, event | category | flops | bytes accessed | tf_op | source)
XLA Modules:
  0.0 178.3 jit_solution(2127741816839808147)
XLA Ops:
  0.6 6.3 %pack_rows.3 = bf16[16,16,4352]{2,1,0:T(8,128)(2,1)} custom-call(s32[1,256]{1,0:T(1,128)} %bin_local.3, s32[1,256]{1,0:T(1,128)} %bin_offset.3, s32[1,256]{1,0:T(1,128)} %spill_node.3, s32[1,256]{1,0:T(1,128)} %spill_offset.3, bf16[256,5120]{1,0:T(8,128)(2,1)} %q.5, bf16[256,5120]{1,0:T(8,128)(2,1)} %g.5, bf16[256,2048]{1,0:T(8,128)(2,1)} %v.1, ...), custom_call_target="tpu_custom_call" | custom-call | flops 570425344 | bytes 14680064 | tf_op jit(solution)/shard_map/pack_rows/pallas_call | solution.py:213
  6.9 11.5 %all-to-all-start = ((bf16[16,16,4352]{2,1,0:T(8,128)(2,1)}), bf16[16,16,4352]{2,1,0:T(8,128)(2,1)}, u32[]{:S(2)}, u32[]{:S(2)}) async-start(bf16[16,16,4352]{2,1,0:T(8,128)(2,1)} %pack_rows.3), calls=%async_computation | async-start | bytes 4456448 | tf_op jit(solution)/shard_map/all_to_all | solution.py:587
  18.4 7.3 %pack_rows.2 = (bf16[16,16,3072]{2,1,0:T(8,128)(2,1)}, bf16[16,16,1408]{2,1,0:T(8,128)(2,1)}) custom-call(s32[1,256]{1,0:T(1,128)} %bin_local.3, s32[1,256]{1,0:T(1,128)} %bin_offset.3, s32[1,256]{1,0:T(1,128)} %spill_node.3, s32[1,256]{1,0:T(1,128)} %spill_offset.3, bf16[256,5120]{1,0:T(8,128)(2,1)} %q.5, bf16[256,5120]{1,0:T(8,128)(2,1)} %g.5, ...), custom_call_target="tpu_custom_call" | custom-call | flops 570425344 | bytes 14680064 | tf_op jit(solution)/shard_map/pack_rows/pallas_call | solution.py:213
  25.7 0.0 copy-start.6
  25.7 28.2 %all-to-all-done.near = bf16[16,16,4352]{2,1,0:T(8,128)(2,1)} async-done(((bf16[16,16,4352]{2,1,0:T(8,128)(2,1)}), bf16[16,16,4352]{2,1,0:T(8,128)(2,1)}, u32[]{:S(2)}, u32[]{:S(2)}) %all-to-all-start) | async-done | bytes 2228256 | tf_op jit(solution)/shard_map/all_to_all | solution.py:587
  53.9 25.4 %all-to-all-start.1 = ((bf16[16,16,3072]{2,1,0:T(8,128)(2,1)}), bf16[16,16,3072]{2,1,0:T(8,128)(2,1)}, u32[]{:S(2)}, u32[]{:S(2)}) async-start(bf16[16,16,3072]{2,1,0:T(8,128)(2,1)} %get-tuple-element.22), calls=%async_computation.1 | async-start | bytes 3145728 | tf_op jit(solution)/shard_map/all_to_all | solution.py:589
  79.3 0.0 copy-start.1
  79.4 0.0 copy-done.6
  79.4 0.2 convert_reduce_fusion.1
  79.6 0.5 multiply_sine_fusion
  80.1 0.8 pad_maximum_fusion
  80.9 1.1 slice.9.near
  82.1 0.0 copy-done
  82.1 0.0 copy-done.1
  82.1 1.9 %near_adapter_rows.1 = (bf16[64,204800]{1,0:T(8,128)(2,1)}, bf16[320,128]{1,0:T(8,128)(2,1)S(1)}) custom-call(bf16[16,16,1280]{2,1,0:T(8,128)(2,1)S(1)} %slice.9.near, bf16[256,5120]{1,0:T(8,128)(2,1)S(1)} %copy-done, bf16[5120,128]{1,0:T(8,128)(2,1)S(1)} %copy-done.1), custom_call_target="tpu_custom_call" | custom-call | flops 83886080 | bytes 9437184 | tf_op jit(solution)/shard_map/near_adapter_rows/pallas_call | solution.py:240
  84.0 28.9 %all-to-all-done.1.far = bf16[16,16,3072]{2,1,0:T(8,128)(2,1)} async-done(((bf16[16,16,3072]{2,1,0:T(8,128)(2,1)}), bf16[16,16,3072]{2,1,0:T(8,128)(2,1)}, u32[]{:S(2)}, u32[]{:S(2)}) %all-to-all-start.1) | async-done | bytes 1572896 | tf_op jit(solution)/shard_map/all_to_all | solution.py:589
  112.9 8.3 %all-to-all-start.2 = ((bf16[16,16,1408]{2,1,0:T(8,128)(2,1)}), bf16[16,16,1408]{2,1,0:T(8,128)(2,1)S(1)}, u32[]{:S(2)}, u32[]{:S(2)}) async-start(bf16[16,16,1408]{2,1,0:T(8,128)(2,1)} %get-tuple-element.27), calls=%async_computation.2 | async-start | bytes 1441792 | tf_op jit(solution)/shard_map/all_to_all | solution.py:597
  121.2 0.0 copy-start.2
  121.2 0.0 copy-start.3
  121.2 0.0 copy-start.4
  121.2 16.5 %attention_grads.1 = (bf16[256,2048]{1,0:T(8,128)(2,1)}, bf16[256,49152]{1,0:T(8,128)(2,1)}) custom-call(s32[1,256]{1,0:T(1,128)} %pick_row.3, s32[1,256]{1,0:T(1,128)} %seg_row.1, f32[256,128]{1,0:T(8,128)} %get-tuple-element.28.cos, f32[256,128]{1,0:T(8,128)} %get-tuple-element.29.sin, bf16[128,1024]{1,0:T(8,128)(2,1)} %up.1, bf16[256,5120]{1,0:T(8,128)(2,1)} %q.5, ...), custom_call_target="tpu_custom_call" | custom-call | flops 12000000000 | bytes 14680064 | tf_op jit(solution)/shard_map/attention_grads/pallas_call | solution.py:359
  137.7 1.4 all-to-all-done.2.far
  139.2 5.2 %adapter_grads.1 = (bf16[16,192,128]{2,1,0:T(8,128)(2,1)S(1)}, bf16[16,192,128]{2,1,0:T(8,128)(2,1)S(1)}, bf16[256,2048]{1,0:T(8,128)(2,1)}) custom-call(s32[1,256]{1,0:T(1,128)S(1)} %copy-done.4, s32[96,1]{1,0:T(8,128)S(1)} %copy-done.3, s32[96,1]{1,0:T(8,128)S(1)} %copy-done.2, ...), custom_call_target="tpu_custom_call", output_to_operand_aliasing={{2}: (8, {})} | custom-call | flops 4000000000 | bytes 10485760 | tf_op jit(solution)/shard_map/adapter_grads/pallas_call | solution.py:503
  144.4 0.1 collective-permute-start
  144.5 2.3 %collective-permute-done = bf16[16,192,128]{2,1,0:T(8,128)(2,1)S(1)} collective-permute-done((bf16[16,192,128]{2,1,0:T(8,128)(2,1)S(1)}, bf16[16,192,128]{2,1,0:T(8,128)(2,1)S(1)}, u32[]{:S(2)}, u32[]{:S(2)}) %collective-permute-start) | collective-permute-done | bytes 786464 | tf_op jit(solution)/shard_map/ppermute | solution.py:548
  146.7 0.2 add_convert_fusion
  146.9 18.7 %all_to_all.25 = bf16[16,192,128]{2,1,0:T(8,128)(2,1)S(1)} all-to-all(bf16[16,192,128]{2,1,0:T(8,128)(2,1)S(1)} %add_convert_fusion), channel_id=1, replica_groups={{0,16,32,48,4,20,36,52,8,24,40,56,12,28,44,60},{1,17,33,49,5,21,37,53,9..., dimensions={0} | all-to-all | bytes 1572864 | tf_op jit(solution)/shard_map/all_to_all | solution.py:537
  165.7 0.1 convert_reduce_fusion
  165.8 11.8 %all_to_all.26 = f32[8,24,128]{2,1,0:T(8,128)S(1)} all-to-all(f32[8,24,128]{2,1,0:T(8,128)S(1)} %bitcast.3), channel_id=1, replica_groups={{0,2,64,66,128,130,192,194},{1,3,65,67,129,131,193,195},{4,6,68,70,132,..., dimensions={0} | all-to-all | bytes 196608 | tf_op jit(solution)/shard_map/all_to_all | solution.py:537
  177.7 0.0 copy-start.5
  177.7 0.6 slice.13
  178.3 0.0 copy-done.5
  (8 shorter events, 0.0 us)
Async XLA Ops:
  6.9 47.0 %all-to-all-start = ((bf16[16,16,4352]{2,1,0:T(8,128)(2,1)}), bf16[16,16,4352]{2,1,0:T(8,128)(2,1)}, u32[]{:S(2)}, u32[]{:S(2)}) async-start(bf16[16,16,4352]{2,1,0:T(8,128)(2,1)} %pack_rows.3), calls=%async_computation | async-start | bytes 4456448 | tf_op jit(solution)/shard_map/all_to_all | solution.py:587
  25.7 53.7 %copy-start.6 = (s32[1,256]{1,0:T(1,128)S(1)}, s32[1,256]{1,0:T(1,128)}, u32[]{:S(2)}) copy-start(s32[1,256]{1,0:T(1,128)} %seg_row.1) | copy-start | bytes 3076
  53.9 28.2 %copy-start = (bf16[256,5120]{1,0:T(8,128)(2,1)S(1)}, bf16[256,5120]{1,0:T(8,128)(2,1)}, u32[]{:S(2)}) copy-start(bf16[256,5120]{1,0:T(8,128)(2,1)} %x.7) | copy-start | bytes 7864324
  53.9 59.0 %all-to-all-start.1 = ((bf16[16,16,3072]{2,1,0:T(8,128)(2,1)}), bf16[16,16,3072]{2,1,0:T(8,128)(2,1)}, u32[]{:S(2)}, u32[]{:S(2)}) async-start(bf16[16,16,3072]{2,1,0:T(8,128)(2,1)} %get-tuple-element.22), calls=%async_computation.1 | async-start | bytes 3145728 | tf_op jit(solution)/shard_map/all_to_all | solution.py:589
  79.3 2.8 %copy-start.1 = (bf16[5120,128]{1,0:T(8,128)(2,1)S(1)}, bf16[5120,128]{1,0:T(8,128)(2,1)}, u32[]{:S(2)}) copy-start(bf16[5120,128]{1,0:T(8,128)(2,1)} %down.1) | copy-start | bytes 3932164
  112.9 26.2 %all-to-all-start.2 = ((bf16[16,16,1408]{2,1,0:T(8,128)(2,1)}), bf16[16,16,1408]{2,1,0:T(8,128)(2,1)S(1)}, u32[]{:S(2)}, u32[]{:S(2)}) async-start(bf16[16,16,1408]{2,1,0:T(8,128)(2,1)} %get-tuple-element.27), calls=%async_computation.2 | async-start | bytes 1441792 | tf_op jit(solution)/shard_map/all_to_all | solution.py:597
  121.2 18.0 %copy-start.2 = (s32[96,1]{1,0:T(8,128)S(1)}, s32[96,1]{1,0:T(8,128)}, u32[]{:S(2)}) copy-start(s32[96,1]{1,0:T(8,128)} %constant.18.clone.core_step) | copy-start | bytes 1156
  121.2 18.0 %copy-start.3 = (s32[96,1]{1,0:T(8,128)S(1)}, s32[96,1]{1,0:T(8,128)}, u32[]{:S(2)}) copy-start(s32[96,1]{1,0:T(8,128)} %constant.17.clone.first_core) | copy-start | bytes 1156
  121.2 18.0 %copy-start.4 = (s32[1,256]{1,0:T(1,128)S(1)}, s32[1,256]{1,0:T(1,128)}, u32[]{:S(2)}) copy-start(s32[1,256]{1,0:T(1,128)} %pick_row.3) | copy-start | bytes 3076
  144.4 2.4 %collective-permute-start = (bf16[16,192,128]{2,1,0:T(8,128)(2,1)S(1)}, bf16[16,192,128]{2,1,0:T(8,128)(2,1)S(1)}, u32[]{:S(2)}, u32[]{:S(2)}) collective-permute-start(bf16[16,192,128]{2,1,0:T(8,128)(2,1)S(1)} %get-tuple-element.36), channel_id=1, source_target_pairs={{0,1},{1,0},{2,3},{3,2},{4,5},{5,4},{6,7},{7,6},{8,9},{9,8},{10,11... | collective-permute-start | bytes 2359304 | tf_op jit(solution)/shard_map/ppermute | solution.py:548
  177.7 0.6 copy-start.5

commit v4 on v3

--- a/solution.py
+++ b/solution.py
@@ -121,7 +121,8 @@
     if not near:
         down_in, att_down, down_sem = rest
         x_loads.append(pltpu.make_async_copy(down, down_in, down_sem.at[0]))
-    for load in loads + x_loads:
+    middle = 1 + KV_HEADS
+    for load in loads[:middle] + x_loads + loads[middle:]:
         load.start()
 
     stays_in = bin_local[...] == lax.axis_index("local")
@@ -137,8 +138,7 @@
         stores.append(pltpu.make_async_copy(source, to, sem))
         stores[-1].start()
 
-    loads[0].wait()
-    for j in range(KV_HEADS):
+    def pack_head(j):
         loads[1 + 2 * j].wait()
         loads[2 + 2 * j].wait()
         part = columns(j, GROUP_WIDTH)
@@ -154,6 +154,10 @@
         part = columns(j, HEAD_QUARTER)
         att[:, :, part] = interleave(dot(select, rows), spread.at[j % 2])
         send(att.at[:, :, part], att_out.at[:, :, part], out_sem.at[j])
+
+    loads[0].wait()
+    for j in range(KV_HEADS // 2):
+        pack_head(j)
     for load in x_loads:
         load.wait()
     moved_down = 0.0
@@ -171,6 +175,8 @@
             moved_down = moved_down + dot(picked.astype(BF), down_rows)
         to = slice(x_from + part.start, x_from + part.stop)
         send(att_x.at[:, :, part], x_out.at[:, :, to], out_sem.at[KV_HEADS + j])
+    for j in range(KV_HEADS // 2, KV_HEADS):
+        pack_head(j)
     if not near:
         picked = moved_down.astype(BF).astype(F32)
         rows = jnp.concatenate([picked] + [jnp.zeros_like(picked)] * (QUARTERS - 1), axis=1)

time: 179 us -> 180 us (level)
  Pallas kernels: 37.1 us -> 39 us
    pallas_call x2, Pallas kernels: 13.5 us -> 15.4 us  [pack(): pl.pallas_call(functools.partial(pack_kernel, near), in_specs=[vmem] * 4...]
  transfers between devices with their start and end apart: 4 -> 4, of which waited for: 4 -> 4; matrix products, arithmetic and copies ran while one was open for 2% -> 2% of each run, Pallas kernels for 14% -> 15%
where the time goes in v4:
time: 180 us; the launch traced here: 179 us
  waiting for transfers between devices  59.9 us (33%)
  starting transfers between devices  45.3 us (25%)
  Pallas kernels  39 us (22%)
  blocking collectives  30.6 us (17%)
  other arithmetic  1.9 us (1%)
    all_to_all x2, blocking collectives, exchange(): lax.all_to_all(array, ('node', 'local'), split_axis=0, concat_axis=0, axi...  30.6 us
    all_to_all x1, waiting for transfers between devices, local(): lax.all_to_all(far_send, 'node', split_axis=0, concat_axis=0, tiled=True)  28.9 us
    all_to_all x1, waiting for transfers between devices, local(): lax.all_to_all(near_send, 'local', split_axis=0, concat_axis=0, tiled=True)  27.3 us
    all_to_all x1, starting transfers between devices, local(): lax.all_to_all(far_send, 'node', split_axis=0, concat_axis=0, tiled=True)  25.4 us
    pallas_call x1, Pallas kernels, attention(): pl.pallas_call(attention_kernel, grid=(KV_HEADS // STEP_HEADS,), in_specs...  16.5 us
    pallas_call x2, Pallas kernels, pack(): pl.pallas_call(functools.partial(pack_kernel, near), in_specs=[vmem] * 4...  15.4 us
    all_to_all x1, starting transfers between devices, local(): lax.all_to_all(near_send, 'local', split_axis=0, concat_axis=0, tiled=True)  11.5 us
    all_to_all x1, starting transfers between devices, local(): lax.all_to_all(far_x_send, 'node', split_axis=0, concat_axis=0, tiled=True)  8.25 us
  transfers between devices with their start and end apart: 4, of which 4 were waited for; matrix products, arithmetic and copies ran while one was open for 2% of the time, Pallas kernels for 15%

profile of v4, /device:TPU:2, one launch (start us, length us, event | category | flops | bytes accessed | tf_op | source)
XLA Modules:
  0.0 179.2 jit_solution(12060027608311492463)
XLA Ops:
  0.6 7.2 %pack_rows.3 = bf16[16,16,4352]{2,1,0:T(8,128)(2,1)} custom-call(s32[1,256]{1,0:T(1,128)} %bin_local.3, s32[1,256]{1,0:T(1,128)} %bin_offset.3, s32[1,256]{1,0:T(1,128)} %spill_node.3, s32[1,256]{1,0:T(1,128)} %spill_offset.3, bf16[256,5120]{1,0:T(8,128)(2,1)} %q.5, bf16[256,5120]{1,0:T(8,128)(2,1)} %g.5, bf16[256,2048]{1,0:T(8,128)(2,1)} %v.1, ...), custom_call_target="tpu_custom_call" | custom-call | flops 570425344 | bytes 14680064 | tf_op jit(solution)/shard_map/pack_rows/pallas_call | solution.py:219
  7.9 11.5 %all-to-all-start = ((bf16[16,16,4352]{2,1,0:T(8,128)(2,1)}), bf16[16,16,4352]{2,1,0:T(8,128)(2,1)}, u32[]{:S(2)}, u32[]{:S(2)}) async-start(bf16[16,16,4352]{2,1,0:T(8,128)(2,1)} %pack_rows.3), calls=%async_computation | async-start | bytes 4456448 | tf_op jit(solution)/shard_map/all_to_all | solution.py:593
  19.3 8.2 %pack_rows.2 = (bf16[16,16,3072]{2,1,0:T(8,128)(2,1)}, bf16[16,16,1408]{2,1,0:T(8,128)(2,1)}) custom-call(s32[1,256]{1,0:T(1,128)} %bin_local.3, s32[1,256]{1,0:T(1,128)} %bin_offset.3, s32[1,256]{1,0:T(1,128)} %spill_node.3, s32[1,256]{1,0:T(1,128)} %spill_offset.3, bf16[256,5120]{1,0:T(8,128)(2,1)} %q.5, bf16[256,5120]{1,0:T(8,128)(2,1)} %g.5, ...), custom_call_target="tpu_custom_call" | custom-call | flops 570425344 | bytes 14680064 | tf_op jit(solution)/shard_map/pack_rows/pallas_call | solution.py:219
  27.6 0.0 copy-start.6
  27.6 27.3 %all-to-all-done.near = bf16[16,16,4352]{2,1,0:T(8,128)(2,1)} async-done(((bf16[16,16,4352]{2,1,0:T(8,128)(2,1)}), bf16[16,16,4352]{2,1,0:T(8,128)(2,1)}, u32[]{:S(2)}, u32[]{:S(2)}) %all-to-all-start) | async-done | bytes 2228256 | tf_op jit(solution)/shard_map/all_to_all | solution.py:593
  54.9 25.4 %all-to-all-start.1 = ((bf16[16,16,3072]{2,1,0:T(8,128)(2,1)}), bf16[16,16,3072]{2,1,0:T(8,128)(2,1)}, u32[]{:S(2)}, u32[]{:S(2)}) async-start(bf16[16,16,3072]{2,1,0:T(8,128)(2,1)} %get-tuple-element.22), calls=%async_computation.1 | async-start | bytes 3145728 | tf_op jit(solution)/shard_map/all_to_all | solution.py:595
  80.3 0.0 copy-start.1
  80.3 0.0 copy-done.6
  80.3 0.2 convert_reduce_fusion.1
  80.5 0.5 multiply_sine_fusion
  81.1 0.8 pad_maximum_fusion
  81.9 1.1 slice.9.near
  83.0 0.0 copy-done
  83.1 1.9 %near_adapter_rows.1 = (bf16[64,204800]{1,0:T(8,128)(2,1)}, bf16[320,128]{1,0:T(8,128)(2,1)S(1)}) custom-call(bf16[16,16,1280]{2,1,0:T(8,128)(2,1)S(1)} %slice.9.near, bf16[256,5120]{1,0:T(8,128)(2,1)S(1)} %copy-done, bf16[5120,128]{1,0:T(8,128)(2,1)S(1)} %copy-done.1), custom_call_target="tpu_custom_call" | custom-call | flops 83886080 | bytes 9437184 | tf_op jit(solution)/shard_map/near_adapter_rows/pallas_call | solution.py:246
  84.9 28.9 %all-to-all-done.1.far = bf16[16,16,3072]{2,1,0:T(8,128)(2,1)} async-done(((bf16[16,16,3072]{2,1,0:T(8,128)(2,1)}), bf16[16,16,3072]{2,1,0:T(8,128)(2,1)}, u32[]{:S(2)}, u32[]{:S(2)}) %all-to-all-start.1) | async-done | bytes 1572896 | tf_op jit(solution)/shard_map/all_to_all | solution.py:595
  113.8 8.3 %all-to-all-start.2 = ((bf16[16,16,1408]{2,1,0:T(8,128)(2,1)}), bf16[16,16,1408]{2,1,0:T(8,128)(2,1)S(1)}, u32[]{:S(2)}, u32[]{:S(2)}) async-start(bf16[16,16,1408]{2,1,0:T(8,128)(2,1)} %get-tuple-element.27), calls=%async_computation.2 | async-start | bytes 1441792 | tf_op jit(solution)/shard_map/all_to_all | solution.py:603
  122.1 0.0 copy-start.2
  122.1 0.0 copy-start.3
  122.1 0.0 copy-start.4
  122.1 16.5 %attention_grads.1 = (bf16[256,2048]{1,0:T(8,128)(2,1)}, bf16[256,49152]{1,0:T(8,128)(2,1)}) custom-call(s32[1,256]{1,0:T(1,128)} %pick_row.3, s32[1,256]{1,0:T(1,128)} %seg_row.1, f32[256,128]{1,0:T(8,128)} %get-tuple-element.28.cos, f32[256,128]{1,0:T(8,128)} %get-tuple-element.29.sin, bf16[128,1024]{1,0:T(8,128)(2,1)} %up.1, bf16[256,5120]{1,0:T(8,128)(2,1)} %q.5, ...), custom_call_target="tpu_custom_call" | custom-call | flops 12000000000 | bytes 14680064 | tf_op jit(solution)/shard_map/attention_grads/pallas_call | solution.py:365
  138.6 1.4 all-to-all-done.2.far
  140.1 0.0 copy-done.4
  140.1 5.2 %adapter_grads.1 = (bf16[16,192,128]{2,1,0:T(8,128)(2,1)S(1)}, bf16[16,192,128]{2,1,0:T(8,128)(2,1)S(1)}, bf16[256,2048]{1,0:T(8,128)(2,1)}) custom-call(s32[1,256]{1,0:T(1,128)S(1)} %copy-done.4, s32[96,1]{1,0:T(8,128)S(1)} %copy-done.3, s32[96,1]{1,0:T(8,128)S(1)} %copy-done.2, ...), custom_call_target="tpu_custom_call", output_to_operand_aliasing={{2}: (8, {})} | custom-call | flops 4000000000 | bytes 10485760 | tf_op jit(solution)/shard_map/adapter_grads/pallas_call | solution.py:509
  145.3 0.1 collective-permute-start
  145.4 2.3 %collective-permute-done = bf16[16,192,128]{2,1,0:T(8,128)(2,1)S(1)} collective-permute-done((bf16[16,192,128]{2,1,0:T(8,128)(2,1)S(1)}, bf16[16,192,128]{2,1,0:T(8,128)(2,1)S(1)}, u32[]{:S(2)}, u32[]{:S(2)}) %collective-permute-start) | collective-permute-done | bytes 786464 | tf_op jit(solution)/shard_map/ppermute | solution.py:554
  147.7 0.2 add_convert_fusion
  147.9 18.8 %all_to_all.25 = bf16[16,192,128]{2,1,0:T(8,128)(2,1)S(1)} all-to-all(bf16[16,192,128]{2,1,0:T(8,128)(2,1)S(1)} %add_convert_fusion), channel_id=1, replica_groups={{0,16,32,48,4,20,36,52,8,24,40,56,12,28,44,60},{1,17,33,49,5,21,37,53,9..., dimensions={0} | all-to-all | bytes 1572864 | tf_op jit(solution)/shard_map/all_to_all | solution.py:543
  166.7 0.1 convert_reduce_fusion
  166.8 11.8 %all_to_all.26 = f32[8,24,128]{2,1,0:T(8,128)S(1)} all-to-all(f32[8,24,128]{2,1,0:T(8,128)S(1)} %bitcast.3), channel_id=1, replica_groups={{0,2,64,66,128,130,192,194},{1,3,65,67,129,131,193,195},{4,6,68,70,132,..., dimensions={0} | all-to-all | bytes 196608 | tf_op jit(solution)/shard_map/all_to_all | solution.py:543
  178.6 0.0 copy-start.5
  178.6 0.6 slice.13
  179.2 0.0 copy-done.5
  (8 shorter events, 0.0 us)
Async XLA Ops:
  7.9 47.0 %all-to-all-start = ((bf16[16,16,4352]{2,1,0:T(8,128)(2,1)}), bf16[16,16,4352]{2,1,0:T(8,128)(2,1)}, u32[]{:S(2)}, u32[]{:S(2)}) async-start(bf16[16,16,4352]{2,1,0:T(8,128)(2,1)} %pack_rows.3), calls=%async_computation | async-start | bytes 4456448 | tf_op jit(solution)/shard_map/all_to_all | solution.py:593
  27.6 52.8 %copy-start.6 = (s32[1,256]{1,0:T(1,128)S(1)}, s32[1,256]{1,0:T(1,128)}, u32[]{:S(2)}) copy-start(s32[1,256]{1,0:T(1,128)} %seg_row.1) | copy-start | bytes 3076
  54.9 28.2 %copy-start = (bf16[256,5120]{1,0:T(8,128)(2,1)S(1)}, bf16[256,5120]{1,0:T(8,128)(2,1)}, u32[]{:S(2)}) copy-start(bf16[256,5120]{1,0:T(8,128)(2,1)} %x.7) | copy-start | bytes 7864324
  54.9 59.0 %all-to-all-start.1 = ((bf16[16,16,3072]{2,1,0:T(8,128)(2,1)}), bf16[16,16,3072]{2,1,0:T(8,128)(2,1)}, u32[]{:S(2)}, u32[]{:S(2)}) async-start(bf16[16,16,3072]{2,1,0:T(8,128)(2,1)} %get-tuple-element.22), calls=%async_computation.1 | async-start | bytes 3145728 | tf_op jit(solution)/shard_map/all_to_all | solution.py:595
  80.3 2.8 %copy-start.1 = (bf16[5120,128]{1,0:T(8,128)(2,1)S(1)}, bf16[5120,128]{1,0:T(8,128)(2,1)}, u32[]{:S(2)}) copy-start(bf16[5120,128]{1,0:T(8,128)(2,1)} %down.1) | copy-start | bytes 3932164
  113.8 26.2 %all-to-all-start.2 = ((bf16[16,16,1408]{2,1,0:T(8,128)(2,1)}), bf16[16,16,1408]{2,1,0:T(8,128)(2,1)S(1)}, u32[]{:S(2)}, u32[]{:S(2)}) async-start(bf16[16,16,1408]{2,1,0:T(8,128)(2,1)} %get-tuple-element.27), calls=%async_computation.2 | async-start | bytes 1441792 | tf_op jit(solution)/shard_map/all_to_all | solution.py:603
  122.1 18.0 %copy-start.2 = (s32[96,1]{1,0:T(8,128)S(1)}, s32[96,1]{1,0:T(8,128)}, u32[]{:S(2)}) copy-start(s32[96,1]{1,0:T(8,128)} %constant.18.clone.core_step) | copy-start | bytes 1156
  122.1 18.0 %copy-start.3 = (s32[96,1]{1,0:T(8,128)S(1)}, s32[96,1]{1,0:T(8,128)}, u32[]{:S(2)}) copy-start(s32[96,1]{1,0:T(8,128)} %constant.17.clone.first_core) | copy-start | bytes 1156
  122.1 18.0 %copy-start.4 = (s32[1,256]{1,0:T(1,128)S(1)}, s32[1,256]{1,0:T(1,128)}, u32[]{:S(2)}) copy-start(s32[1,256]{1,0:T(1,128)} %pick_row.3) | copy-start | bytes 3076
  145.3 2.4 %collective-permute-start = (bf16[16,192,128]{2,1,0:T(8,128)(2,1)S(1)}, bf16[16,192,128]{2,1,0:T(8,128)(2,1)S(1)}, u32[]{:S(2)}, u32[]{:S(2)}) collective-permute-start(bf16[16,192,128]{2,1,0:T(8,128)(2,1)S(1)} %get-tuple-element.36), channel_id=1, source_target_pairs={{0,1},{1,0},{2,3},{3,2},{4,5},{5,4},{6,7},{7,6},{8,9},{9,8},{10,11... | collective-permute-start | bytes 2359304 | tf_op jit(solution)/shard_map/ppermute | solution.py:554
  178.6 0.6 copy-start.5
